TPU v7x, 512 devices: a whole 4x4x16 slice. The times are simulated.
512 devices in a mesh: dp: 2 (over y_lo), group: 32 (over z, core), head: 8 (over x, y_hi).
Axes of the slice: x: 4, y: 4 (y_hi: 2, y_lo: 2; y = y_hi * 2 + y_lo), z: 16, core: 2. Of those that a mesh axis runs over, the one named last changes fastest.
Arguments:
- prefix_kv: bfloat16 [2, 1536, 8, 256], P('dp', 'group', 'head'), may hold values from -6 to 6
- comp_q: bfloat16 [2, 32, 128, 5120], P('dp', 'group', None, 'head'), may hold values from -12 to 12
- comp_kv: bfloat16 [2, 32, 128, 8, 256], P('dp', 'group', None, 'head'), may hold values from -6 to 6
- grad_out: bfloat16 [2, 32, 128, 5120], P('dp', 'group', None, 'head'), may hold values from -6 to 6
- rewards: float32 [2, 32], P('dp', 'group'), may hold values from -6 to 6
- lengths: int32 [2, 32], P('dp', 'group'), may hold values from 32 to 128, as said below
- deal: int32 [2, 32, 32], P('dp', 'group'), may hold values from 0 to 31, each once within a row
Outputs:
- packed_attn: bfloat16 [2, 32, 32, 4, 5120], P('dp', 'group', 'head')
- grad_q: bfloat16 [2, 32, 128, 5120], P('dp', 'group', None, 'head')
- grad_comp_kv: bfloat16 [2, 32, 128, 8, 256], P('dp', 'group', None, 'head')
- grad_prefix_kv: bfloat16 [2, 1536, 8, 256], P('dp', 'group', 'head')
Inputs may be any that keep to these rules, and one draw needn't show every extreme that they name: `lengths`: each completion's live rows are the first ones of its 128 slots; every prompt has a completion of exactly 128 live rows. `deal`: for each completion the last dimension is a permutation of the 32 trainers.
All inputs are finite; a program needn't handle non-finite values.
Results may differ from a plain program's by a relative error of at most 0.011.
Values may be sent and summed in bfloat16 or wider, within the bound.
A program may use at most 64 MiB of HBM per device.

v0:
```python
import math

import jax
import jax.numpy as jnp
from jax import lax
from jax.sharding import PartitionSpec as P


def product(left, right):
    return jnp.dot(left, right, preferred_element_type=jnp.float32)


def product_nt(left, right):
    return lax.dot_general(
        left, right, (((1,), (1,)), ((), ())), preferred_element_type=jnp.float32
    )


def product_tn(left, right):
    return lax.dot_general(
        left, right, (((0,), (0,)), ((), ())), preferred_element_type=jnp.float32
    )


def body(prefix_kv, comp_q, comp_kv, grad_out, rewards, lengths, deal):
    depth = comp_kv.shape[-1] // 2
    slots = comp_q.shape[2]
    heads = comp_q.shape[3] // depth
    groups = lax.axis_size("group")
    scale = 1.0 / math.sqrt(depth)
    own_reward = rewards[0, 0]
    own_length = lengths[0, 0]
    reward_sum = lax.psum(own_reward, "group")
    live_total = lax.psum(own_length.astype(jnp.float32), ("dp", "group"))
    advantage = own_reward - reward_sum / groups
    weight = advantage * (lax.axis_size("dp") * groups * slots) / live_total
    whole_prefix = lax.all_gather(prefix_kv[0, :, 0, :], "group", axis=0, tiled=True)
    prefix_keys = whole_prefix[:, :depth]
    prefix_values = whole_prefix[:, depth:]
    own_keys = comp_kv[0, 0, :, 0, :depth]
    own_values = comp_kv[0, 0, :, 0, depth:]
    positions = lax.iota(jnp.int32, slots)
    causal = positions[:, None] >= positions[None, :]
    live = (positions < own_length)[:, None]
    prompt_rows = whole_prefix.shape[0]
    saved_queries, saved_grads, saved_highest, saved_totals, saved_deltas = ([], [], [], [], [])
    attn_parts, query_parts = ([], [])
    key_grad = jnp.zeros((slots, depth), jnp.float32)
    value_grad = jnp.zeros((slots, depth), jnp.float32)
    prefix_key_grad = jnp.zeros((prompt_rows, depth), jnp.float32)
    prefix_value_grad = jnp.zeros((prompt_rows, depth), jnp.float32)
    for head in range(heads):
        query = comp_q[0, 0, :, head * depth : (head + 1) * depth]
        prefix_scores = product_nt(query, prefix_keys) * scale
        own_scores = jnp.where(causal, product_nt(query, own_keys) * scale, -jnp.inf)
        highest = jnp.maximum(jnp.max(prefix_scores, axis=1), jnp.max(own_scores, axis=1))[:, None]
        prefix_exp = jnp.exp(prefix_scores - highest)
        own_exp = jnp.exp(own_scores - highest)
        total = (jnp.sum(prefix_exp, axis=1) + jnp.sum(own_exp, axis=1))[:, None]
        prefix_probs = prefix_exp / total
        own_probs = own_exp / total
        prefix_half = prefix_probs.astype(jnp.bfloat16)
        own_half = own_probs.astype(jnp.bfloat16)
        attn = product(prefix_half, prefix_values) + product(own_half, own_values)
        attn = lax.optimization_barrier(jnp.where(live, attn, 0.0).astype(jnp.bfloat16))
        out_grad = grad_out[0, 0, :, head * depth : (head + 1) * depth].astype(jnp.float32) * weight
        out_grad = lax.optimization_barrier(jnp.where(live, out_grad, 0.0).astype(jnp.bfloat16))
        delta = jnp.sum(
            out_grad.astype(jnp.float32) * attn.astype(jnp.float32), axis=1, keepdims=True
        )
        prefix_dscores = (prefix_probs * (product_nt(out_grad, prefix_values) - delta)).astype(
            jnp.bfloat16
        )
        own_dscores = (own_probs * (product_nt(out_grad, own_values) - delta)).astype(jnp.bfloat16)
        query_grad = (product(prefix_dscores, prefix_keys) + product(own_dscores, own_keys)) * scale
        key_grad = key_grad + product_tn(own_dscores, query) * scale
        value_grad = value_grad + product_tn(own_half, out_grad)
        prefix_key_grad = prefix_key_grad + product_tn(prefix_dscores, query) * scale
        prefix_value_grad = prefix_value_grad + product_tn(prefix_half, out_grad)
        attn_parts.append(attn)
        query_parts.append(query_grad.astype(jnp.bfloat16))
        saved_queries.append(query)
        saved_grads.append(out_grad)
        saved_highest.append(highest)
        saved_totals.append(total)
        saved_deltas.append(delta)
    term = jnp.concatenate([prefix_key_grad, prefix_value_grad], axis=1)
    prefix_grad = lax.psum_scatter(term, "group", scatter_dimension=0, tiled=True)
    spread = jnp.concatenate(attn_parts, axis=1).reshape(slots // groups, groups, heads * depth)
    route = (deal[0, 0][None, :] == lax.iota(jnp.int32, groups)[:, None]).astype(jnp.bfloat16)
    outgoing = jnp.einsum("tj,mjf->tmf", route, spread, preferred_element_type=jnp.float32).astype(
        jnp.bfloat16
    )
    arrived = lax.all_to_all(
        lax.all_to_all(outgoing, "group", split_axis=0, concat_axis=0, tiled=True),
        "head",
        split_axis=0,
        concat_axis=2,
        tiled=True,
    )
    query_out = jnp.concatenate(query_parts, axis=1)
    comp_out = jnp.concatenate([key_grad, value_grad], axis=1).astype(jnp.bfloat16)
    prefix_out = prefix_grad.astype(jnp.bfloat16)
    return (
        arrived[None, None],
        query_out[None, None],
        comp_out[None, None, :, None, :],
        prefix_out[None, :, None, :],
    )


def solution(mesh):
    placed = (
        P("dp", "group", "head", None),
        P("dp", "group", None, "head"),
        P("dp", "group", None, "head", None),
        P("dp", "group", None, "head"),
        P("dp", "group"),
        P("dp", "group"),
        P("dp", "group", None),
    )
    return jax.shard_map(
        body,
        mesh=mesh,
        in_specs=placed,
        out_specs=(
            P("dp", "group", "head", None, None),
            P("dp", "group", None, "head"),
            P("dp", "group", None, "head", None),
            P("dp", "group", "head", None),
        ),
        check_vma=False,
    )
```

profile of v0, /device:TPU:1, one launch (start us, length us, event | category | flops | bytes accessed | tf_op | source)
XLA Modules:
  0.0 347.5 jit_solution(9129702055253759420)
XLA Ops:
  7.2 1.6 fusion.234
  8.8 1.0 fusion.236
  9.8 1.0 fusion.238
  10.7 1.0 fusion.240
  11.7 1.0 fusion.242
  12.7 40.0 %all-gather = bf16[1,1536,1,256]{3,1,2,0:T(8,128)(2,1)S(1)} all-gather(bf16[1,48,1,256]{3,1,2,0:T(8,128)(2,1)} %param.7), channel_id=2, replica_groups=mesh['dp'=2,'group'=32,'head'=8] {'group'}, dimensions={1}, use_global_device_ids=true | all-gather | bytes 811008 | tf_op jit(solution)/shard_map/all_gather | solution.py:37
  52.7 1.1 fusion.235
  54.5 1.2 fusion.241
  55.7 1.1 fusion.233
  63.8 0.8 copy.20
  64.5 7.0 %all-to-all-start = ((bf16[32,4,640]{2,1,0:T(4,128)(2,1)}), bf16[32,4,640]{2,1,0:T(4,128)(2,1)}, u32[]{:S(2)}, u32[]{:S(2)}) async-start(bf16[32,4,640]{2,1,0:T(4,128)(2,1)} %copy.20), calls=%async_computation | async-start | bytes 327680 | tf_op jit(solution)/shard_map/all_to_all | solution.py:95
  71.6 106.7 %psum.15 = f32[]{:T(128)} all-reduce(f32[]{:T(128)S(6)} %convert_element_type.190), channel_id=1, replica_groups=mesh['dp'=2,'group'=32,'head'=8] {'dp','group'}, use_global_device_ids=true, to_apply=%region_21.22 | all-reduce | flops 1 | bytes 8 | tf_op jit(solution)/shard_map/psum | solution.py:34
  178.9 49.2 %psum.14 = f32[]{:T(128)} all-reduce(f32[]{:T(128)} %bitcast.14), channel_id=1, replica_groups=mesh['dp'=2,'group'=32,'head'=8] {'group'}, use_global_device_ids=true, to_apply=%region_20.21 | all-reduce | flops 1 | bytes 8 | tf_op jit(solution)/shard_map/psum | solution.py:33
  229.6 1.5 fusion.78
  234.0 0.8 copy-done.3
  240.0 1.6 copy.35
  245.8 0.7 copy.28
  249.1 6.4 %all-to-all-start.1 = ((bf16[32,4,640]{2,1,0:T(4,128)(2,1)}), bf16[32,4,640]{2,1,0:T(4,128)(2,1)S(1)}, u32[]{:S(2)}, u32[]{:S(2)}) async-start(bf16[32,4,640]{2,1,0:T(4,128)(2,1)} %all-to-all-done), calls=%async_computation.1 | async-start | bytes 327680 | tf_op jit(solution)/shard_map/all_to_all | solution.py:94
  255.6 0.8 copy.27
  256.5 5.9 %all-to-all-done.1 = bf16[32,4,640]{2,1,0:T(4,128)(2,1)S(1)} async-done(((bf16[32,4,640]{2,1,0:T(4,128)(2,1)}), bf16[32,4,640]{2,1,0:T(4,128)(2,1)S(1)}, u32[]{:S(2)}, u32[]{:S(2)}) %all-to-all-start.1) | async-done | bytes 163872 | tf_op jit(solution)/shard_map/all_to_all | solution.py:94
  262.4 0.7 broadcast_in_dim.88
  263.1 75.9 %reduce-scatter.4.cloned.1.call-done = f32[48,256]{1,0:T(8,128)} async-done(((f32[1536,256]{1,0:T(8,128)}), f32[48,256]{1,0:T(8,128)}) %reduce-scatter.4.cloned.1.call-update) | async-done | bytes 49168
  339.0 0.9 copy.36
  339.9 0.7 copy.29
  (223 shorter events, 21.3 us)
Async XLA Ops:
  7.2 46.6 %copy-start.12 = (bf16[1,1,128,640]{3,2,1,0:T(8,128)(2,1)S(1)}, bf16[1,1,128,640]{3,2,1,0:T(8,128)(2,1)}, u32[]{:S(2)}) copy-start(bf16[1,1,128,640]{3,2,1,0:T(8,128)(2,1)} %param.8) | copy-start | bytes 491524
  9.7 48.4 %copy-start.34 = (f32[128,128]{0,1:T(8,128)}, f32[128,128]{0,1:T(8,128)S(1)}, u32[]{:S(2)}) copy-start(f32[128,128]{0,1:T(8,128)S(1)} %get-tuple-element.24) | copy-start | bytes 196612
  10.7 48.8 %copy-start.32 = (f32[128,128]{0,1:T(8,128)}, f32[128,128]{0,1:T(8,128)S(1)}, u32[]{:S(2)}) copy-start(f32[128,128]{0,1:T(8,128)S(1)} %get-tuple-element.28) | copy-start | bytes 196612
  11.7 48.7 %copy-start.30 = (f32[128,128]{0,1:T(8,128)}, f32[128,128]{0,1:T(8,128)S(1)}, u32[]{:S(2)}) copy-start(f32[128,128]{0,1:T(8,128)S(1)} %get-tuple-element.32) | copy-start | bytes 196612
  12.7 49.1 %copy-start.28 = (f32[128,128]{0,1:T(8,128)}, f32[128,128]{0,1:T(8,128)S(1)}, u32[]{:S(2)}) copy-start(f32[128,128]{0,1:T(8,128)S(1)} %get-tuple-element.36) | copy-start | bytes 196612
  57.8 173.4 %copy-start.55 = (f32[128]{0:T(128)}, f32[128]{0:T(128)S(1)}, u32[]{:S(2)}) copy-start(f32[128]{0:T(128)S(1)} %add.121) | copy-start | bytes 1540
  59.2 172.7 %copy-start.52 = (f32[128]{0:T(128)}, f32[128]{0:T(128)S(1)}, u32[]{:S(2)}) copy-start(f32[128]{0:T(128)S(1)} %add.123) | copy-start | bytes 1540
  60.1 172.4 %copy-start.58 = (f32[128]{0:T(128)}, f32[128]{0:T(128)S(1)}, u32[]{:S(2)}) copy-start(f32[128]{0:T(128)S(1)} %add.125) | copy-start | bytes 1540
  61.5 171.7 %copy-start.61 = (f32[128]{0:T(128)}, f32[128]{0:T(128)S(1)}, u32[]{:S(2)}) copy-start(f32[128]{0:T(128)S(1)} %add.127) | copy-start | bytes 1540
  62.1 167.5 %copy-start.38 = (f32[128]{0:T(128)}, f32[128]{0:T(128)S(1)}, u32[]{:S(2)}) copy-start(f32[128]{0:T(128)S(1)} %max.35) | copy-start | bytes 1540
  62.9 166.6 %copy-start.64 = (f32[128]{0:T(128)}, f32[128]{0:T(128)S(1)}, u32[]{:S(2)}) copy-start(f32[128]{0:T(128)S(1)} %add.119) | copy-start | bytes 1540
  63.3 166.0 %copy-start.17 = (bf16[1,1,128,640]{3,2,1,0:T(8,128)(2,1)S(1)}, bf16[1,1,128,640]{3,2,1,0:T(8,128)(2,1)}, u32[]{:S(2)}) copy-start(bf16[1,1,128,640]{3,2,1,0:T(8,128)(2,1)} %param.10) | copy-start | bytes 491524
  64.5 184.5 %all-to-all-start = ((bf16[32,4,640]{2,1,0:T(4,128)(2,1)}), bf16[32,4,640]{2,1,0:T(4,128)(2,1)}, u32[]{:S(2)}, u32[]{:S(2)}) async-start(bf16[32,4,640]{2,1,0:T(4,128)(2,1)} %copy.20), calls=%async_computation | async-start | bytes 327680 | tf_op jit(solution)/shard_map/all_to_all | solution.py:95
  71.5 267.5 %reduce-scatter.4.cloned.1.call-start = ((), (), s32[]{:S(2)}) async-start(), calls=%async_computation.3 | async-start | bytes 1622016
  229.4 4.6 %copy-start.26 = (bf16[128,128]{1,0:T(8,128)(2,1)}, bf16[128,128]{1,0:T(8,128)(2,1)S(1)}, u32[]{:S(2)}) copy-start(bf16[128,128]{1,0:T(8,128)(2,1)S(1)} %get-tuple-element.15) | copy-start | bytes 98308
  229.4 5.8 %copy-start.24 = (bf16[128,128]{1,0:T(8,128)(2,1)}, bf16[128,128]{1,0:T(8,128)(2,1)S(1)}, u32[]{:S(2)}) copy-start(bf16[128,128]{1,0:T(8,128)(2,1)S(1)} %get-tuple-element.14) | copy-start | bytes 98308
  229.4 6.5 %copy-start.22 = (bf16[128,128]{1,0:T(8,128)(2,1)}, bf16[128,128]{1,0:T(8,128)(2,1)S(1)}, u32[]{:S(2)}) copy-start(bf16[128,128]{1,0:T(8,128)(2,1)S(1)} %get-tuple-element.13) | copy-start | bytes 98308
  229.4 7.1 %copy-start.20 = (bf16[128,128]{1,0:T(8,128)(2,1)}, bf16[128,128]{1,0:T(8,128)(2,1)S(1)}, u32[]{:S(2)}) copy-start(bf16[128,128]{1,0:T(8,128)(2,1)S(1)} %get-tuple-element.16) | copy-start | bytes 98308
  229.4 7.7 %copy-start.18 = (bf16[128,128]{1,0:T(8,128)(2,1)}, bf16[128,128]{1,0:T(8,128)(2,1)S(1)}, u32[]{:S(2)}) copy-start(bf16[128,128]{1,0:T(8,128)(2,1)S(1)} %get-tuple-element.12) | copy-start | bytes 98308
  231.7 6.9 %copy-start.10 = (bf16[128,1536]{1,0:T(8,128)(2,1)}, bf16[128,1536]{1,0:T(8,128)(2,1)S(1)}, u32[]{:S(2)}) copy-start(bf16[128,1536]{1,0:T(8,128)(2,1)S(1)} %fusion.7) | copy-start | bytes 1179652
  232.3 6.6 %copy-start.6 = (bf16[128,1536]{1,0:T(8,128)(2,1)}, bf16[128,1536]{1,0:T(8,128)(2,1)S(1)}, u32[]{:S(2)}) copy-start(bf16[128,1536]{1,0:T(8,128)(2,1)S(1)} %fusion.8) | copy-start | bytes 1179652
  233.0 6.2 %copy-start.8 = (bf16[128,1536]{1,0:T(8,128)(2,1)}, bf16[128,1536]{1,0:T(8,128)(2,1)S(1)}, u32[]{:S(2)}) copy-start(bf16[128,1536]{1,0:T(8,128)(2,1)S(1)} %fusion.9) | copy-start | bytes 1179652
  234.8 4.8 %copy-start.4 = (bf16[128,1536]{1,0:T(8,128)(2,1)}, bf16[128,1536]{1,0:T(8,128)(2,1)S(1)}, u32[]{:S(2)}) copy-start(bf16[128,1536]{1,0:T(8,128)(2,1)S(1)} %fusion.10) | copy-start | bytes 1179652
  249.1 13.3 %all-to-all-start.1 = ((bf16[32,4,640]{2,1,0:T(4,128)(2,1)}), bf16[32,4,640]{2,1,0:T(4,128)(2,1)S(1)}, u32[]{:S(2)}, u32[]{:S(2)}) async-start(bf16[32,4,640]{2,1,0:T(4,128)(2,1)} %all-to-all-done), calls=%async_computation.1 | async-start | bytes 327680 | tf_op jit(solution)/shard_map/all_to_all | solution.py:94
  (46 other events, 58.0 us)
Sparse Core Ops, SparseCore 0:
  242.0 96.9 reduce-scatter.3
where the time goes:
time: 351 us; the launch traced here: 347 us
  blocking collectives  196 us (56%)
  waiting for transfers between devices  81.8 us (23%)
  matrix products  23.9 us (7%)
  between operations  17.8 us (5%)
  starting transfers between devices  13.4 us (4%)
  local copies, waits for them, and re-layouts  12.5 us (4%)
    psum x1, blocking collectives, body(): live_total = lax.psum(own_length.astype(jnp.float32), ('dp', 'group'))  107 us
    unnamed x2, waiting for transfers between devices  75.9 us
    psum x1, blocking collectives, body(): reward_sum = lax.psum(own_reward, 'group')  49.2 us
    all_gather x1, blocking collectives, body(): lax.all_gather(prefix_kv[0, :, 0, :], 'group', axis=0, tiled=True)  40 us
    dot_general x20, matrix products, product_nt(): lax.dot_general(left, right, (((1,), (1,)), ((), ())), preferred_element_...  11.9 us
    unnamed x143, local copies, waits for them, and re-layouts  10.9 us
  transfers between devices with their start and end apart: 3, of which 2 were waited for; matrix products, arithmetic and copies ran while one was open for 5% of the time, Pallas kernels for 0%

commit v1 on v0

v1 whole, which is shorter than its diff:
```python
import functools
import math

import jax
import jax.numpy as jnp
from jax import lax
from jax.experimental import pallas as pl
from jax.experimental.pallas import tpu as pltpu
from jax.sharding import PartitionSpec as P

MESH = pl.DeviceIdType.MESH
F32 = jnp.float32
BF16 = jnp.bfloat16


def dot_nn(left, right):
    return jnp.dot(left, right, preferred_element_type=F32)


def dot_nt(left, right):
    return lax.dot_general(left, right, (((1,), (1,)), ((), ())), preferred_element_type=F32)


def dot_tn(left, right):
    return lax.dot_general(left, right, (((0,), (0,)), ((), ())), preferred_element_type=F32)


def kernel(
    sizes,
    pkv,
    q,
    ckv,
    go,
    rew,
    length,
    deal,
    packed,
    grad_q,
    grad_comp,
    grad_prefix,
    kv,
    qs,
    gs,
    gt,
    st,
    dpt,
    dst,
    top,
    acc,
    sc_send,
    sc_recv,
    dp_send,
    dp_recv,
    a2a_send,
    own,
    pair_send,
    pair_recv,
    ring_send,
    ring_recv,
    ag_ss,
    ag_rs,
    sib_ss,
    sib_rs,
    sc_ss,
    sc_rs,
    dp_sem,
    a2a_ss,
    a2a_rs,
    pair_ss,
    pair_rs,
    ring_ss,
    ring_rs,
):
    dps, groups, kvh, hd, slots, nh = sizes
    chips = groups // 2
    half = chips // 2
    shard = pkv.shape[0]
    chunk = 2 * shard
    prompt = groups * shard
    most = slots // groups
    per = groups // kvh
    wide = nh * hd
    scale = 1.0 / math.sqrt(hd)
    rate = scale * math.log2(math.e)

    p = lax.axis_index("dp")
    g = lax.axis_index("group")
    h = lax.axis_index("head")
    z, k = lax.div(g, 2), lax.rem(g, 2)
    right = lax.rem(z + 1, chips) * 2 + k
    left = lax.rem(z + chips - 1, chips) * 2 + k
    sibling = z * 2 + 1 - k
    seat = lax.div(g, per)
    selfish = jnp.where(seat == h, 1, 0)

    barrier = pltpu.get_barrier_semaphore()

    def greet_group(i, _):
        pl.semaphore_signal(
            barrier, inc=1, device_id=(p, lax.rem(g + i, groups), h), device_id_type=MESH
        )
        return 0

    lax.fori_loop(1, groups, greet_group, 0)

    def greet_sender(i, _):
        c, hh = h * per + lax.div(i, kvh), lax.rem(i, kvh)

        @pl.when(jnp.logical_or(c != g, hh != h))
        def _():
            pl.semaphore_signal(barrier, inc=1, device_id=(p, c, hh), device_id_type=MESH)

        return 0

    lax.fori_loop(0, per * kvh, greet_sender, 0)
    pl.semaphore_signal(barrier, inc=1, device_id=(1 - p, g, h), device_id_type=MESH)
    pl.semaphore_wait(barrier, 2 * groups - selfish)

    def shard_ref(zz, kk):
        return kv.at[pl.ds(pl.multiple_of((zz * 2 + kk) * shard, shard), shard), :]

    def around(step, direction):
        there = right if direction == 0 else left
        from_z = lax.rem(z + (chips - step if direction == 0 else step), chips)
        return pltpu.make_async_remote_copy(
            src_ref=shard_ref(from_z, k),
            dst_ref=shard_ref(from_z, k),
            send_sem=ag_ss.at[direction, step],
            recv_sem=ag_rs.at[direction, step],
            device_id=(p, there, h),
            device_id_type=MESH,
        )

    def arrival(step, direction):
        there = right if direction == 0 else left
        from_z = lax.rem(z + (chips - step - 1 if direction == 0 else step + 1), chips)
        return pltpu.make_async_remote_copy(
            src_ref=shard_ref(from_z, k),
            dst_ref=shard_ref(from_z, k),
            send_sem=ag_ss.at[direction, step],
            recv_sem=ag_rs.at[direction, step],
            device_id=(p, there, h),
            device_id_type=MESH,
        )

    def to_sibling(off, kk):
        zz = lax.rem(z + chips - off, chips)
        return pltpu.make_async_remote_copy(
            src_ref=shard_ref(zz, kk),
            dst_ref=shard_ref(zz, kk),
            send_sem=sib_ss.at[off],
            recv_sem=sib_rs.at[off],
            device_id=(p, sibling, h),
            device_id_type=MESH,
        )

    kv[pl.ds(pl.multiple_of(g * shard, shard), shard), :] = pkv[...]
    around(0, 0).start()
    around(0, 1).start()
    to_sibling(0, k).start()

    lane = lax.broadcasted_iota(jnp.int32, (1, hd), 1)
    reward = rew[0, 0]
    live_rows = length[0, 0]
    facts = jnp.where(lane < hd // 2, reward, live_rows.astype(F32))
    sc_send[...] = facts

    def scalar_copy(i):
        return pltpu.make_async_remote_copy(
            src_ref=sc_send,
            dst_ref=sc_recv.at[i],
            send_sem=sc_ss.at[i],
            recv_sem=sc_rs.at[i],
            device_id=(p, lax.rem(g + i, groups), h),
            device_id_type=MESH,
        )

    def send_scalar(i, _):
        scalar_copy(i).start()
        return 0

    lax.fori_loop(1, groups, send_scalar, 0)

    row = lax.broadcasted_iota(jnp.int32, (slots, hd), 0)
    for j in range(nh):
        cols = slice(j * hd, (j + 1) * hd)
        rows = slice(j * slots, (j + 1) * slots)
        qs[rows, :] = q[:, cols]
        grad = jnp.where(row < live_rows, go[:, cols].astype(F32), 0.0)
        gs[rows, :] = grad.astype(BF16)
        gt[:, rows] = grad.T
    kv[prompt:, :] = ckv[...]

    key_at = lax.broadcasted_iota(jnp.int32, (slots, wide), 0)
    query_at = lax.broadcasted_iota(jnp.int32, (slots, wide), 1) & (slots - 1)
    own_scores = jnp.where(key_at <= query_at, dot_nt(ckv[:, :hd], qs[...]), -1e30)
    st[prompt:, :] = own_scores
    dpt[prompt:, :] = dot_nt(ckv[:, hd:], gs[...])
    top[...] = jnp.max(own_scores, axis=0, keepdims=True)

    def chunk_rows(zz):
        return pl.ds(pl.multiple_of(zz * chunk, chunk), chunk)

    def scores(off):
        rows = chunk_rows(lax.rem(z + chips - off, chips))
        s = dot_nt(kv[rows, :hd], qs[...])
        st[rows, :] = s
        top[...] = jnp.maximum(top[...], jnp.max(s, axis=0, keepdims=True))
        dpt[rows, :] = dot_nt(kv[rows, hd:], gs[...])

    def receive(off):
        to_sibling(off, 1 - k).wait_recv()

    receive(0)
    scores(0)

    def gather(s, _):
        arrival(s - 1, 0).wait_recv()
        around(s, 0).start()
        to_sibling(s, k).start()
        arrival(s - 1, 1).wait_recv()

        @pl.when(s < half - 1)
        def _():
            around(s, 1).start()

        to_sibling(chips - s, k).start()
        receive(s)
        scores(s)
        receive(chips - s)
        scores(chips - s)
        return 0

    lax.fori_loop(1, half, gather, 0)
    arrival(half - 1, 0).wait_recv()
    to_sibling(half, k).start()
    receive(half)
    scores(half)

    def wait_scalar(i, _):
        scalar_copy(i).wait_recv()
        return 0

    lax.fori_loop(1, groups, wait_scalar, 0)
    sums = facts + jnp.sum(sc_recv[1:], axis=0)
    dp_send[...] = sums
    other = pltpu.make_async_remote_copy(
        src_ref=dp_send,
        dst_ref=dp_recv,
        send_sem=dp_sem.at[0],
        recv_sem=dp_sem.at[1],
        device_id=(1 - p, g, h),
        device_id_type=MESH,
    )
    other.start()

    highest = top[...] * rate
    acc[...] = jnp.zeros_like(acc)

    def exponents(rows, total):
        e = jnp.exp2(st[rows, :] * rate - highest)
        st[rows, :] = e
        acc[...] += dot_tn(kv[rows, hd:], e.astype(BF16))
        return total + jnp.sum(e, axis=0, keepdims=True)

    block = prompt // 3

    def some_exponents(i, total):
        return exponents(pl.ds(pl.multiple_of(i * block, block), block), total)

    total = exponents(pl.ds(prompt, slots), jnp.zeros((1, wide), F32))
    total = lax.fori_loop(0, prompt // block, some_exponents, total)
    inverse = 1.0 / total
    col = lax.broadcasted_iota(jnp.int32, (1, wide), 1) & (slots - 1)
    attn_t = jnp.where(col < live_rows, acc[...] * inverse, 0.0).astype(BF16)
    delta = jnp.sum(gt[...] * attn_t.astype(F32), axis=0, keepdims=True)

    to_row = lax.broadcasted_iota(jnp.int32, (slots, slots), 0)
    from_row = lax.broadcasted_iota(jnp.int32, (slots, slots), 1)
    dealt = jnp.concatenate([deal[...]] * most, axis=1)
    route = jnp.where(
        jnp.logical_and(
            (to_row & (most - 1)) == lax.shift_right_logical(from_row, int(math.log2(groups))),
            lax.shift_right_logical(to_row, int(math.log2(most))) == dealt,
        ),
        1.0,
        0.0,
    ).astype(BF16)
    for j in range(nh):
        cols = slice(j * hd, (j + 1) * hd)
        moved = dot_nt(route, attn_t[:, cols])
        for t in range(groups):
            a2a_send[t, :, cols] = moved[t * most : (t + 1) * most, :].astype(BF16)

    def place(c, hh):
        return packed.at[lax.rem(c, per), :, pl.ds(pl.multiple_of(hh * wide, wide), wide)]

    my_place = lax.rem(g, per) * kvh + h

    def send_rows(i, _):
        t = lax.rem(g + i, groups)
        mine = jnp.logical_and(t == g, seat == h)

        @pl.when(mine)
        def _():
            pltpu.make_async_copy(a2a_send.at[t], place(g, h), a2a_rs.at[my_place]).start()

        @pl.when(jnp.logical_not(mine))
        def _():
            pltpu.make_async_remote_copy(
                src_ref=a2a_send.at[t],
                dst_ref=place(g, h),
                send_sem=a2a_ss.at[i],
                recv_sem=a2a_rs.at[my_place],
                device_id=(p, t, seat),
                device_id_type=MESH,
            ).start()

        return 0

    lax.fori_loop(0, groups, send_rows, 0)

    other.wait_recv()
    live_total = sums[:, hd - 1 :] + dp_recv[:, hd - 1 :]
    advantage = facts[:, :1] - sums[:, :1] / groups
    weight = advantage * (dps * groups * slots) / live_total
    key_weight = weight * scale

    def gradients(rows):
        probs = st[rows, :] * inverse
        ds = (probs * (dpt[rows, :] - delta)).astype(BF16)
        dst[rows, :] = ds
        key_grad = dot_nn(ds, qs[...]) * key_weight
        value_grad = dot_nn(probs.astype(BF16), gs[...]) * weight
        return key_grad, value_grad

    def pair_copy(off):
        return pltpu.make_async_remote_copy(
            src_ref=pair_send.at[off, pl.ds(pl.multiple_of((1 - k) * shard, shard), shard), :],
            dst_ref=pair_recv.at[off],
            send_sem=pair_ss.at[off],
            recv_sem=pair_rs.at[off],
            device_id=(p, sibling, h),
            device_id_type=MESH,
        )

    def prepare(off, slot):
        key_grad, value_grad = gradients(chunk_rows(lax.rem(z + off, chips)))
        own[slot, :, :hd] = key_grad
        own[slot, :, hd:] = value_grad
        pair_send[off, :, :hd] = key_grad.astype(BF16)
        pair_send[off, :, hd:] = value_grad.astype(BF16)
        pair_copy(off).start()

    def pair_sum(off, slot):
        pair_copy(off).wait_recv()
        mine = own[slot, pl.ds(pl.multiple_of(k * shard, shard), shard), :]
        return mine + pair_recv[off].astype(F32)

    def ring_copy(s, direction):
        return pltpu.make_async_remote_copy(
            src_ref=ring_send.at[direction, s],
            dst_ref=ring_recv.at[direction, s],
            send_sem=ring_ss.at[direction, s],
            recv_sem=ring_rs.at[direction, s],
            device_id=(p, right if direction == 0 else left, h),
            device_id_type=MESH,
        )

    def ring_off(s, direction):
        return half - s if direction == 0 else half + 1 + s

    def pass_on(s, direction):
        term = pair_sum(ring_off(s, direction), direction)

        @pl.when(s == 0)
        def _():
            ring_send[direction, s] = term.astype(BF16)

        @pl.when(s > 0)
        def _():
            ring_copy(s - 1, direction).wait_recv()
            ring_send[direction, s] = (term + ring_recv[direction, s - 1].astype(F32)).astype(BF16)

        ring_copy(s, direction).start()

    prepare(ring_off(0, 0), 0)
    prepare(ring_off(0, 1), 1)

    def scatter(s, _):
        pass_on(s, 0)
        pass_on(s, 1)
        prepare(ring_off(s + 1, 0), 0)

        @pl.when(s < half - 2)
        def _():
            prepare(ring_off(s + 1, 1), 1)

        return 0

    lax.fori_loop(0, half - 1, scatter, 0)
    pass_on(half - 1, 0)
    prepare(0, 1)

    key_grad, value_grad = gradients(pl.ds(prompt, slots))
    grad_comp[:, :hd] = key_grad.astype(BF16)
    grad_comp[:, hd:] = value_grad.astype(BF16)
    query_grad = dot_tn(kv[:, :hd], dst[...]) * key_weight
    for j in range(nh):
        cols = slice(j * hd, (j + 1) * hd)
        grad_q[:, cols] = query_grad[:, cols].T.astype(BF16)

    term = pair_sum(0, 1)
    ring_copy(half - 2, 1).wait_recv()
    term = term + ring_recv[1, half - 2].astype(F32)
    ring_copy(half - 1, 0).wait_recv()
    grad_prefix[...] = (term + ring_recv[0, half - 1].astype(F32)).astype(BF16)

    def wait_rows(i, _):
        c, hh = lax.div(i, kvh), lax.rem(i, kvh)
        pltpu.make_async_copy(a2a_send.at[0], place(c, hh), a2a_rs.at[i]).wait()
        return 0

    lax.fori_loop(0, groups, wait_rows, 0)

    def wait_sent(i, _):
        t = lax.rem(g + i, groups)

        @pl.when(jnp.logical_not(jnp.logical_and(t == g, seat == h)))
        def _():
            pltpu.make_async_remote_copy(
                src_ref=a2a_send.at[t],
                dst_ref=place(g, h),
                send_sem=a2a_ss.at[i],
                recv_sem=a2a_rs.at[my_place],
                device_id=(p, t, seat),
                device_id_type=MESH,
            ).wait_send()

        @pl.when(i > 0)
        def _():
            scalar_copy(i).wait_send()

        return 0

    lax.fori_loop(0, groups, wait_sent, 0)
    other.wait_send()

    def wait_steps(s, _):
        around(s, 0).wait_send()
        ring_copy(s, 0).wait_send()

        @pl.when(s < half - 1)
        def _():
            around(s, 1).wait_send()
            ring_copy(s, 1).wait_send()

        return 0

    lax.fori_loop(0, half, wait_steps, 0)

    def wait_pairs(off, _):
        to_sibling(off, k).wait_send()
        pair_copy(off).wait_send()
        return 0

    lax.fori_loop(0, chips, wait_pairs, 0)


def body(prefix_kv, comp_q, comp_kv, grad_out, rewards, lengths, deal):
    hd = comp_kv.shape[-1] // 2
    slots = comp_q.shape[2]
    wide = comp_q.shape[3]
    nh = wide // hd
    dps, groups, kvh = (lax.axis_size(name) for name in ("dp", "group", "head"))
    shard = prefix_kv.shape[1]
    prompt = groups * shard
    keys = prompt + slots
    chips = groups // 2
    half = chips // 2
    most = slots // groups
    per = groups // kvh
    vmem = pl.BlockSpec(memory_space=pltpu.VMEM)
    smem = pl.BlockSpec(memory_space=pltpu.SMEM)
    dma = pltpu.SemaphoreType.DMA
    packed, query_out, comp_out, prefix_out = pl.pallas_call(
        functools.partial(kernel, (dps, groups, kvh, hd, slots, nh)),
        out_shape=(
            jax.ShapeDtypeStruct((per, most, kvh * wide), BF16),
            jax.ShapeDtypeStruct((slots, wide), BF16),
            jax.ShapeDtypeStruct((slots, 2 * hd), BF16),
            jax.ShapeDtypeStruct((shard, 2 * hd), BF16),
        ),
        in_specs=[vmem, vmem, vmem, vmem, smem, smem, vmem],
        out_specs=(pl.BlockSpec(memory_space=pl.ANY), vmem, vmem, vmem),
        scratch_shapes=[
            pltpu.VMEM((keys, 2 * hd), BF16),
            pltpu.VMEM((nh * slots, hd), BF16),
            pltpu.VMEM((nh * slots, hd), BF16),
            pltpu.VMEM((hd, nh * slots), F32),
            pltpu.VMEM((keys, nh * slots), F32),
            pltpu.VMEM((keys, nh * slots), F32),
            pltpu.VMEM((keys, nh * slots), BF16),
            pltpu.VMEM((1, nh * slots), F32),
            pltpu.VMEM((hd, nh * slots), F32),
            pltpu.VMEM((1, hd), F32),
            pltpu.VMEM((groups, 1, hd), F32),
            pltpu.VMEM((1, hd), F32),
            pltpu.VMEM((1, hd), F32),
            pltpu.VMEM((groups, most, wide), BF16),
            pltpu.VMEM((2, 2 * shard, 2 * hd), F32),
            pltpu.VMEM((chips, 2 * shard, 2 * hd), BF16),
            pltpu.VMEM((chips, shard, 2 * hd), BF16),
            pltpu.VMEM((2, half, shard, 2 * hd), BF16),
            pltpu.VMEM((2, half, shard, 2 * hd), BF16),
            dma((2, half)),
            dma((2, half)),
            dma((chips,)),
            dma((chips,)),
            dma((groups,)),
            dma((groups,)),
            dma((2,)),
            dma((groups,)),
            dma((groups,)),
            dma((chips,)),
            dma((chips,)),
            dma((2, half)),
            dma((2, half)),
        ],
        compiler_params=pltpu.CompilerParams(
            collective_id=0, has_side_effects=True, vmem_limit_bytes=48 * 2**20
        ),
        name="shared_prompt_attention",
    )(
        prefix_kv[0, :, 0, :],
        comp_q[0, 0],
        comp_kv[0, 0, :, 0, :],
        grad_out[0, 0],
        rewards,
        lengths,
        deal[0],
    )
    return (
        packed[None, None],
        query_out[None, None],
        comp_out[None, None, :, None, :],
        prefix_out[None, :, None, :],
    )


def solution(mesh):
    placed = (
        P("dp", "group", "head", None),
        P("dp", "group", None, "head"),
        P("dp", "group", None, "head", None),
        P("dp", "group", None, "head"),
        P("dp", "group"),
        P("dp", "group"),
        P("dp", "group", None),
    )
    return jax.shard_map(
        body,
        mesh=mesh,
        in_specs=placed,
        out_specs=(
            P("dp", "group", "head", None, None),
            P("dp", "group", None, "head"),
            P("dp", "group", None, "head", None),
            P("dp", "group", "head", None),
        ),
        check_vma=False,
    )
```

time: 351 us -> 86.1 us (0.25)
  blocking collectives: 196 us -> 0 us
  waiting for transfers between devices: 81.8 us -> 0 us
  Pallas kernels: 0 us -> 77.2 us
  matrix products: 23.9 us -> 0 us
  between operations: 17.8 us -> 1.95 us
  starting transfers between devices: 13.4 us -> 0 us
  local copies, waits for them, and re-layouts: 12.5 us -> 6.63 us
    psum x2 -> x0, blocking collectives: 156 us -> none  [the longest x1 107 us: body(): live_total = lax.psum(own_length.astype(jnp.float32), ('dp', 'group'))]
    pallas_call x0 -> x1, Pallas kernels: none -> 77.2 us  [body(): pl.pallas_call(functools.partial(kernel, (dps, groups, kvh, hd, slots, nh...]
    unnamed x2 -> x0, waiting for transfers between devices: 75.9 us -> none
    all_gather x1 -> x0, blocking collectives: 40 us -> none  [body(): lax.all_gather(prefix_kv[0, :, 0, :], 'group', axis=0, tiled=True)]
    dot_general x61 -> x0, matrix products: 23.9 us -> none  [the longest x20 11.9 us: product_nt(): lax.dot_general(left, right, (((1,), (1,)), ((), ())), preferred_element_...]
    all_to_all x2 -> x0, starting transfers between devices: 13.3 us -> none  [the longest x1 6.98 us: body(): lax.all_to_all(outgoing, 'group', split_axis=0, concat_axis=0, tiled=True)]
    all_to_all x2 -> x0, waiting for transfers between devices: 5.91 us -> none  [the longest x1 5.91 us: body(): lax.all_to_all(lax.all_to_all(outgoing, 'group', split_axis=0, concat_axi...]
    unnamed x143 -> x14, local copies, waits for them, and re-layouts: 10.9 us -> 6.63 us
  transfers between devices with their start and end apart: 3 -> 0, of which waited for: 2 -> 0; matrix products, arithmetic and copies ran while one was open for 5% -> 0% of each run, Pallas kernels for 0% -> 0%
where the time goes in v1:
time: 86.1 us; the launch traced here: 85.8 us
  Pallas kernels  77.2 us (90%)
  local copies, waits for them, and re-layouts  6.63 us (8%)
  between operations  1.95 us (2%)
    pallas_call x1, Pallas kernels, body(): pl.pallas_call(functools.partial(kernel, (dps, groups, kvh, hd, slots, nh...  77.2 us
    unnamed x14, local copies, waits for them, and re-layouts  6.63 us

profile of v1, /device:TPU:1, one launch (start us, length us, event | category | flops | bytes accessed | tf_op | source)
XLA Modules:
  0.0 85.8 jit_solution(15962458999483766893)
XLA Ops:
  1.9 0.0 copy-start.4
  1.9 0.6 copy-done.4
  2.6 0.0 copy-start
  2.6 0.9 %copy-done = bf16[1,1,128,640]{3,2,1,0:T(8,128)(2,1)S(1)} copy-done((bf16[1,1,128,640]{3,2,1,0:T(8,128)(2,1)S(1)}, bf16[1,1,128,640]{3,2,1,0:T(8,128)(2,1)}, u32[]{:S(2)}) %copy-start) | copy-done | bytes 163864
  3.5 0.0 copy-start.1
  3.5 0.9 %copy-done.1 = bf16[1,1,128,640]{3,2,1,0:T(8,128)(2,1)S(1)} copy-done((bf16[1,1,128,640]{3,2,1,0:T(8,128)(2,1)S(1)}, bf16[1,1,128,640]{3,2,1,0:T(8,128)(2,1)}, u32[]{:S(2)}) %copy-start.1) | copy-done | bytes 163864
  4.4 0.0 copy-start.2
  4.4 0.8 copy-done.2
  5.3 0.0 copy-start.3
  5.3 0.7 copy-done.3
  6.0 77.2 %shared_prompt_attention.1 = (bf16[4,4,5120]{2,1,0:T(4,128)(2,1)S(1)}, bf16[128,640]{1,0:T(8,128)(2,1)S(1)}, bf16[128,256]{1,0:T(8,128)(2,1)S(1)}, bf16[48,256]{1,0:T(8,128)(2,1)S(1)}) custom-call(bf16[48,256]{1,0:T(8,128)(2,1)S(1)} %bitcast.15, bf16[128,640]{1,0:T(8,128)(2,1)S(1)} %bitcast.9, bf16[128,256]{1,0:T(8,128)(2,1)S(1)} %bitcast.13, ...), custom_call_target="tpu_custom_call" | custom-call | tf_op jit(solution)/shard_map/shared_prompt_attention/pallas_call | solution.py:486
  83.2 0.7 copy.17
  83.9 0.7 copy.18
  84.6 0.6 copy.19
  85.2 0.6 copy.20
Async XLA Ops:
  1.9 0.7 copy-start.4
  2.6 0.9 %copy-start = (bf16[1,1,128,640]{3,2,1,0:T(8,128)(2,1)S(1)}, bf16[1,1,128,640]{3,2,1,0:T(8,128)(2,1)}, u32[]{:S(2)}) copy-start(bf16[1,1,128,640]{3,2,1,0:T(8,128)(2,1)} %param.8) | copy-start | bytes 491524
  3.5 0.9 %copy-start.1 = (bf16[1,1,128,640]{3,2,1,0:T(8,128)(2,1)S(1)}, bf16[1,1,128,640]{3,2,1,0:T(8,128)(2,1)}, u32[]{:S(2)}) copy-start(bf16[1,1,128,640]{3,2,1,0:T(8,128)(2,1)} %param.10) | copy-start | bytes 491524
  4.4 0.8 copy-start.2
  5.3 0.7 copy-start.3

commit v2 on v1

v2 whole, which is shorter than its diff:
```python
import functools
import math

import jax
import jax.numpy as jnp
from jax import lax
from jax.experimental import pallas as pl
from jax.experimental.pallas import tpu as pltpu
from jax.sharding import PartitionSpec as P

MESH = pl.DeviceIdType.MESH
F32 = jnp.float32
BF16 = jnp.bfloat16
NEAR = (5, -5, 3, -3, 2, -2, 1, -1)
RELAY = 5
FAR = 8
VMEM = 64 * 2**20


def dot_nn(left, right):
    return jnp.dot(left, right, preferred_element_type=F32)


def dot_nt(left, right):
    return lax.dot_general(left, right, (((1,), (1,)), ((), ())), preferred_element_type=F32)


def dot_tn(left, right):
    return lax.dot_general(left, right, (((0,), (0,)), ((), ())), preferred_element_type=F32)


def kernel(
    sizes,
    pkv_in,
    q_in,
    ckv_in,
    go_in,
    rew_in,
    length_in,
    deal_in,
    packed,
    grad_q,
    grad_comp,
    grad_prefix,
    q,
    go,
    rew,
    length,
    deal,
    kv,
    qs,
    gs,
    gt,
    st,
    dpt,
    dst,
    top,
    acc,
    sc_send,
    sc_recv,
    a2a_send,
    own,
    pair_send,
    pair_recv,
    tree_send,
    tree_recv,
    in_sems,
    ag_ss,
    ag_rs,
    sib_ss,
    sib_rs,
    sc_ss,
    sc_rs,
    a2a_ss,
    a2a_rs,
    pair_ss,
    pair_rs,
    tree_ss,
    tree_rs,
):
    dps, groups, kvh, hd, slots, nh = sizes
    chips = groups // 2
    shard = pkv_in.shape[0]
    chunk = 2 * shard
    prompt = groups * shard
    most = slots // groups
    per = groups // kvh
    wide = nh * hd
    scale = 1.0 / math.sqrt(hd)
    rate = scale * math.log2(math.e)

    p = lax.axis_index("dp")
    g = lax.axis_index("group")
    h = lax.axis_index("head")
    z, k = lax.div(g, 2), lax.rem(g, 2)
    seat = lax.div(g, per)

    def chip(step):
        return lax.rem(z + step + chips, chips)

    def device(step):
        return (p, chip(step) * 2 + k, h)

    sibling = (p, z * 2 + 1 - k, h)
    across = (1 - p, g, h)

    def shard_rows(zz, kk):
        return pl.ds(pl.multiple_of((zz * 2 + kk) * shard, shard), shard)

    fetches = [
        pltpu.make_async_copy(source, target, in_sems.at[i])
        for i, (source, target) in enumerate(
            (
                (pkv_in, kv.at[shard_rows(z, k), :]),
                (rew_in, rew),
                (length_in, length),
                (go_in, go),
                (q_in, q),
                (ckv_in, kv.at[pl.ds(prompt, slots), :]),
                (deal_in, deal),
            )
        )
    ]
    for fetch in fetches:
        fetch.start()

    barrier = pltpu.get_barrier_semaphore()
    near = [device(step) for step in NEAR]
    for partner in near[:2]:
        pl.semaphore_signal(barrier, inc=1, device_id=partner, device_id_type=MESH)

    def greet_head(i, _):
        partner = (p, g, lax.rem(h + i, kvh))
        pl.semaphore_signal(barrier, inc=1, device_id=partner, device_id_type=MESH)
        return 0

    lax.fori_loop(1, kvh, greet_head, 0)
    for partner in near[2:] + [across, sibling]:
        pl.semaphore_signal(barrier, inc=1, device_id=partner, device_id_type=MESH)
    fetches[0].wait()
    pl.semaphore_wait(barrier, len(near) + 1 + kvh)

    def around(off, step, half=None):
        lanes = slice(None) if half is None else pl.ds(half * hd, hd)
        there = (off + step + chips) % chips
        ref = kv.at[shard_rows(chip(-off), k), lanes]
        return pltpu.make_async_remote_copy(
            src_ref=ref,
            dst_ref=ref,
            send_sem=ag_ss.at[there if half is None else chips + half],
            recv_sem=ag_rs.at[there if half is None else chips + half],
            device_id=device(step),
            device_id_type=MESH,
        )

    def arrived(off):
        rows = shard_rows(chip(-off), k)
        parts = [(slice(None), off)]
        if off == chips // 2:
            parts = [(pl.ds(half * hd, hd), chips + half) for half in range(2)]
        for lanes, sem in parts:
            ref = kv.at[rows, lanes]
            pltpu.make_async_remote_copy(
                src_ref=ref,
                dst_ref=ref,
                send_sem=ag_ss.at[sem],
                recv_sem=ag_rs.at[sem],
                device_id=sibling,
                device_id_type=MESH,
            ).wait_recv()

    def to_sibling(off, kk):
        ref = kv.at[shard_rows(chip(-off), kk), :]
        return pltpu.make_async_remote_copy(
            src_ref=ref,
            dst_ref=ref,
            send_sem=sib_ss.at[off],
            recv_sem=sib_rs.at[off],
            device_id=sibling,
            device_id_type=MESH,
        )

    sent = [around(0, step) for step in (5, -5, 1, -1, 2, -2)]
    for copy in sent[:2]:
        copy.start()
    to_sibling(0, k).start()
    for copy in sent[2:]:
        copy.start()

    lane = lax.broadcasted_iota(jnp.int32, (1, hd), 1)
    fetches[1].wait()
    fetches[2].wait()
    live_rows = length[...]
    facts = jnp.where(lane < hd // 2, rew[...], live_rows.astype(F32))

    def tell(slot, row, target):
        return pltpu.make_async_remote_copy(
            src_ref=sc_send.at[row],
            dst_ref=sc_recv.at[slot],
            send_sem=sc_ss.at[slot],
            recv_sem=sc_rs.at[slot],
            device_id=target,
            device_id_type=MESH,
        )

    sc_send[0] = facts
    told = [tell(1 + i, 0, device(step)) for i, step in enumerate((1, -1, 2, -2, -3))]
    for copy in told:
        copy.start()

    row = lax.broadcasted_iota(jnp.int32, (slots, hd), 0)
    fetches[3].wait()
    for j in range(nh):
        cols = slice(j * hd, (j + 1) * hd)
        rows = slice(j * slots, (j + 1) * slots)
        grad = jnp.where(row < live_rows, go[:, cols].astype(F32), 0.0)
        gs[rows, :] = grad.astype(BF16)
        gt[:, rows] = grad.T
    fetches[4].wait()
    for j in range(nh):
        qs[j * slots : (j + 1) * slots, :] = q[:, j * hd : (j + 1) * hd]
    fetches[5].wait()

    key_at = lax.broadcasted_iota(jnp.int32, (slots, wide), 0)
    query_at = lax.broadcasted_iota(jnp.int32, (slots, wide), 1) & (slots - 1)
    own_rows = pl.ds(prompt, slots)
    own_scores = jnp.where(key_at <= query_at, dot_nt(kv[own_rows, :hd], qs[...]), -1e30)
    st[own_rows, :] = own_scores
    dpt[own_rows, :] = dot_nt(kv[own_rows, hd:], gs[...])
    top[...] = jnp.max(own_scores, axis=0, keepdims=True)

    def chunk_rows(zz):
        return pl.ds(pl.multiple_of(zz * chunk, chunk), chunk)

    def scores(off):
        to_sibling(off, 1 - k).wait_recv()
        rows = chunk_rows(chip(-off))
        s = dot_nt(kv[rows, :hd], qs[...])
        st[rows, :] = s
        top[...] = jnp.maximum(top[...], jnp.max(s, axis=0, keepdims=True))
        dpt[rows, :] = dot_nt(kv[rows, hd:], gs[...])

    def each(count, off_of):
        def one(i, _):
            scores(off_of(i))
            return 0

        lax.fori_loop(0, count, one, 0)

    for off in (1, 15, 2, 14):
        arrived(off)
        to_sibling(off, k).start()
    each(3, lambda i: lax.rem(i + chips - 1, chips))

    for off, steps, far, half in ((5, (1, -1, 2, -2), 3, 0), (11, (-1, 1, -2, 2), -3, 1)):
        arrived(off)
        passed = [around(off, step) for step in steps] + [around(off, far, half)]
        for copy in passed:
            copy.start()
        to_sibling(off, k).start()
        sent += passed

    for copy in told:
        copy.wait_recv()
    window = facts + sc_recv[1] + sc_recv[2] + sc_recv[3] + sc_recv[4]
    sc_send[1] = window + sc_recv[5]
    sc_send[2] = window
    told += [tell(6, 1, device(-5)), tell(7, 2, device(5))]
    for copy in told[5:]:
        copy.start()
    each(2, lambda i: 2 + 12 * i)
    each(2, lambda i: 5 + 6 * i)

    for off in (4, 12, 6, 10, 3, 13, 7, 9):
        arrived(off)
        to_sibling(off, k).start()
    each(4, lambda i: 4 + 2 * i + 2 * lax.div(i, 2))
    arrived(chips // 2)
    to_sibling(chips // 2, k).start()
    for copy in told[5:]:
        copy.wait_recv()
    window = window + sc_recv[6] + sc_recv[7]
    sc_send[3] = window
    told.append(tell(8, 3, sibling))
    told[7].start()
    each(4, lambda i: 3 + 4 * i - 2 * lax.div(i, 2))
    scores(chips // 2)

    highest = top[...] * rate
    acc[...] = jnp.zeros_like(acc)

    def exponents(rows, total):
        e = jnp.exp2(st[rows, :] * rate - highest)
        st[rows, :] = e
        acc[...] += dot_tn(kv[rows, hd:], e.astype(BF16))
        return total + jnp.sum(e, axis=0, keepdims=True)

    block = prompt // 3

    def some_exponents(i, total):
        return exponents(pl.ds(pl.multiple_of(i * block, block), block), total)

    total = exponents(own_rows, jnp.zeros((1, wide), F32))
    total = lax.fori_loop(0, prompt // block, some_exponents, total)
    inverse = 1.0 / total
    col = lax.broadcasted_iota(jnp.int32, (1, wide), 1) & (slots - 1)
    attn_t = jnp.where(col < live_rows, acc[...] * inverse, 0.0).astype(BF16)
    delta = jnp.sum(gt[...] * attn_t.astype(F32), axis=0, keepdims=True)

    told[7].wait_recv()
    sums = window + sc_recv[8]
    sc_send[4] = sums
    told.append(tell(0, 4, across))
    told[8].start()
    weight = (facts[:, :1] - sums[:, :1] / groups) * (dps * groups * slots)
    key_weight = weight * scale

    def gradients(rows):
        probs = st[rows, :] * inverse
        ds = (probs * (dpt[rows, :] - delta)).astype(BF16)
        dst[rows, :] = ds
        key_grad = dot_nn(ds, qs[...]) * key_weight
        value_grad = dot_nn(probs.astype(BF16), gs[...]) * weight
        return key_grad, value_grad

    def pair_copy(off):
        return pltpu.make_async_remote_copy(
            src_ref=pair_send.at[off, pl.ds(pl.multiple_of((1 - k) * shard, shard), shard), :],
            dst_ref=pair_recv.at[off],
            send_sem=pair_ss.at[off],
            recv_sem=pair_rs.at[off],
            device_id=sibling,
            device_id_type=MESH,
        )

    def prepare(off):
        key_grad, value_grad = gradients(chunk_rows(chip(off)))
        own[off, :, :hd] = key_grad
        own[off, :, hd:] = value_grad
        pair_send[off, :, :hd] = key_grad.astype(BF16)
        pair_send[off, :, hd:] = value_grad.astype(BF16)
        pair_copy(off).start()

    def pair_sum(off):
        pair_copy(off).wait_recv()
        mine = own[off, pl.ds(pl.multiple_of(k * shard, shard), shard), :]
        return mine + pair_recv[off].astype(F32)

    def tree_copy(side, far, step):
        return pltpu.make_async_remote_copy(
            src_ref=tree_send.at[side, far],
            dst_ref=tree_recv.at[side, far],
            send_sem=tree_ss.at[side, far],
            recv_sem=tree_rs.at[side, far],
            device_id=device(step),
            device_id_type=MESH,
        )

    def half_copy(side):
        lanes = pl.ds(side * hd, hd)
        return pltpu.make_async_remote_copy(
            src_ref=tree_send.at[0, FAR, :, lanes],
            dst_ref=tree_recv.at[side, FAR, :, lanes],
            send_sem=tree_ss.at[side, FAR],
            recv_sem=tree_rs.at[side, FAR],
            device_id=device(-3 if side == 0 else 3),
            device_id_type=MESH,
        )

    def ship(far, side):
        step = 5 * lax.div(far + 5, 8) - far
        tree_send[side, far] = pair_sum(chips - far if side == 0 else far).astype(BF16)
        tree_copy(side, far, step if side == 0 else -step).start()

    prepare(FAR)

    def leaves(i, _):
        for far in (7 - i, 3 + i):
            prepare(chips - far)
            prepare(far)

        @pl.when(i == 0)
        def _():
            tree_send[0, FAR] = pair_sum(FAR).astype(BF16)
            half_copy(0).start()
            half_copy(1).start()

        @pl.when(i == 1)
        def _():
            for far in (7, 3):
                ship(far, 0)
                ship(far, 1)

        return 0

    lax.fori_loop(0, 2, leaves, 0)

    to_row = lax.broadcasted_iota(jnp.int32, (slots, slots), 0)
    from_row = lax.broadcasted_iota(jnp.int32, (slots, slots), 1)
    fetches[6].wait()
    dealt = jnp.concatenate([deal[...]] * most, axis=1)
    route = jnp.where(
        jnp.logical_and(
            (to_row & (most - 1)) == lax.shift_right_logical(from_row, int(math.log2(groups))),
            lax.shift_right_logical(to_row, int(math.log2(most))) == dealt,
        ),
        1.0,
        0.0,
    ).astype(BF16)
    for j in range(nh):
        cols = slice(j * hd, (j + 1) * hd)
        moved = dot_nt(route, attn_t[:, cols])
        for t in range(groups):
            a2a_send[t, :, cols] = moved[t * most : (t + 1) * most, :].astype(BF16)

    for far in (6, 4):
        ship(far, 0)
        ship(far, 1)

    def place(c, hh):
        return packed.at[lax.rem(c, per), :, pl.ds(pl.multiple_of(hh * wide, wide), wide)]

    def rows_copy(i):
        j = lax.div(i + 1, 2)
        t = lax.rem(g + groups // 2 + j * (1 - 2 * lax.rem(i, 2)), groups)
        return pltpu.make_async_remote_copy(
            src_ref=a2a_send.at[t],
            dst_ref=place(g, h),
            send_sem=a2a_ss,
            recv_sem=a2a_rs,
            device_id=(p, t, seat),
            device_id_type=MESH,
        )

    def send_rows(i, _):
        mine = jnp.logical_and(i == groups - 1, seat == h)

        @pl.when(mine)
        def _():
            pltpu.make_async_copy(a2a_send.at[g], place(g, h), a2a_rs).start()

        @pl.when(jnp.logical_not(mine))
        def _():
            rows_copy(i).start()

        return 0

    lax.fori_loop(0, groups, send_rows, 0)

    def nearer(i, _):
        far = RELAY - 3 * lax.div(i + 1, 2) - lax.div(i, 2)
        prepare(chips - far)
        prepare(far)

        @pl.when(i == 2)
        def _():
            ship(2, 0)
            ship(2, 1)

        return 0

    lax.fori_loop(0, 3, nearer, 0)
    ship(1, 0)
    ship(1, 1)
    prepare(0)

    for side in range(2):
        term = pair_sum(chips - RELAY if side == 0 else RELAY)
        for far in (7, 6, 4, 3):
            tree_copy(side, far, 1).wait_recv()
            term = term + tree_recv[side, far].astype(F32)
        half_copy(side).wait_recv()
        lanes = slice(side * hd, (side + 1) * hd)
        rest = slice((1 - side) * hd, (2 - side) * hd)
        tree_send[side, RELAY, :, lanes] = (
            term[:, lanes] + tree_recv[side, FAR, :, lanes].astype(F32)
        ).astype(BF16)
        tree_send[side, RELAY, :, rest] = term[:, rest].astype(BF16)
        tree_copy(side, RELAY, -5 if side == 0 else 5).start()

    key_grad, value_grad = gradients(own_rows)
    query_grad = dot_tn(kv[:, :hd], dst[...]) * key_weight
    told[8].wait_recv()
    share = 1.0 / (sums[:, hd - 1 :] + sc_recv[0][:, hd - 1 :])
    grad_comp[:, :hd] = (key_grad * share).astype(BF16)
    grad_comp[:, hd:] = (value_grad * share).astype(BF16)
    for j in range(nh):
        cols = slice(j * hd, (j + 1) * hd)
        grad_q[:, cols] = (query_grad[:, cols] * share).T.astype(BF16)

    for copy in sent + told:
        copy.wait_send()

    def wait_pairs(off, _):
        to_sibling(off, k).wait_send()
        pair_copy(off).wait_send()
        return 0

    lax.fori_loop(0, chips, wait_pairs, 0)

    def wait_far(far, _):
        for side in range(2):
            tree_copy(side, far, 1).wait_send()
        return 0

    lax.fori_loop(1, FAR, wait_far, 0)
    for side in range(2):
        half_copy(side).wait_send()

    term = pair_sum(0)
    for far in (2, 1, RELAY):
        for side in range(2):
            tree_copy(side, far, 1).wait_recv()
            term = term + tree_recv[side, far].astype(F32)
    grad_prefix[...] = (term * share).astype(BF16)

    pltpu.make_async_copy(packed, packed, a2a_rs).wait()
    for held in range(2):
        part = a2a_send.at[pl.ds(0, groups - held)]

        @pl.when((seat == h) == (held == 1))
        def _():
            pltpu.make_async_copy(part, part, a2a_ss).wait()


def hand_over(*refs):
    count = (len(refs) - 1) // 2
    copies = [pltpu.make_async_copy(refs[i], refs[count + i], refs[-1].at[i]) for i in range(count)]
    for copy in copies:
        copy.start()
    for copy in copies:
        copy.wait()


def body(prefix_kv, comp_q, comp_kv, grad_out, rewards, lengths, deal):
    hd = comp_kv.shape[-1] // 2
    slots = comp_q.shape[2]
    wide = comp_q.shape[3]
    nh = wide // hd
    dps, groups, kvh = (lax.axis_size(name) for name in ("dp", "group", "head"))
    shard = prefix_kv.shape[1]
    prompt = groups * shard
    keys = prompt + slots
    chips = groups // 2
    most = slots // groups
    per = groups // kvh
    assert chips == 16
    vmem = pl.BlockSpec(memory_space=pltpu.VMEM)
    anywhere = pl.BlockSpec(memory_space=pl.ANY)
    dma = pltpu.SemaphoreType.DMA
    made = pl.pallas_call(
        functools.partial(kernel, (dps, groups, kvh, hd, slots, nh)),
        out_shape=(
            jax.ShapeDtypeStruct((per, most, kvh * wide), BF16),
            jax.ShapeDtypeStruct((slots, wide), BF16),
            jax.ShapeDtypeStruct((slots, 2 * hd), BF16),
            jax.ShapeDtypeStruct((shard, 2 * hd), BF16),
        ),
        in_specs=[anywhere] * 7,
        out_specs=(anywhere, vmem, vmem, vmem),
        scratch_shapes=[
            pltpu.VMEM((slots, wide), BF16),
            pltpu.VMEM((slots, wide), BF16),
            pltpu.VMEM((1, 1), F32),
            pltpu.VMEM((1, 1), jnp.int32),
            pltpu.VMEM((1, groups), jnp.int32),
            pltpu.VMEM((keys, 2 * hd), BF16),
            pltpu.VMEM((nh * slots, hd), BF16),
            pltpu.VMEM((nh * slots, hd), BF16),
            pltpu.VMEM((hd, nh * slots), F32),
            pltpu.VMEM((keys, nh * slots), F32),
            pltpu.VMEM((keys, nh * slots), F32),
            pltpu.VMEM((keys, nh * slots), BF16),
            pltpu.VMEM((1, nh * slots), F32),
            pltpu.VMEM((hd, nh * slots), F32),
            pltpu.VMEM((5, 1, hd), F32),
            pltpu.VMEM((9, 1, hd), F32),
            pltpu.VMEM((groups, most, wide), BF16),
            pltpu.VMEM((chips, 2 * shard, 2 * hd), F32),
            pltpu.VMEM((chips, 2 * shard, 2 * hd), BF16),
            pltpu.VMEM((chips, shard, 2 * hd), BF16),
            pltpu.VMEM((2, FAR + 1, shard, 2 * hd), BF16),
            pltpu.VMEM((2, FAR + 1, shard, 2 * hd), BF16),
            dma((7,)),
            dma((chips + 2,)),
            dma((chips + 2,)),
            dma((chips,)),
            dma((chips,)),
            dma((9,)),
            dma((9,)),
            dma,
            dma,
            dma((chips,)),
            dma((chips,)),
            dma((2, FAR + 1)),
            dma((2, FAR + 1)),
        ],
        compiler_params=pltpu.CompilerParams(
            collective_id=0, has_side_effects=True, vmem_limit_bytes=VMEM
        ),
        name="shared_prompt_attention",
    )(
        prefix_kv[0, :, 0, :],
        comp_q[0, 0],
        comp_kv[0, 0, :, 0, :],
        grad_out[0, 0],
        rewards,
        lengths,
        deal[0],
    )
    packed, query_out, comp_out, prefix_out = pl.pallas_call(
        hand_over,
        out_shape=tuple(jax.ShapeDtypeStruct(x.shape, x.dtype) for x in made),
        in_specs=[anywhere] * len(made),
        out_specs=(anywhere,) * len(made),
        scratch_shapes=[dma((len(made),))],
        compiler_params=pltpu.CompilerParams(vmem_limit_bytes=VMEM),
        name="hand_over",
    )(*made)
    return (
        packed[None, None],
        query_out[None, None],
        comp_out[None, None, :, None, :],
        prefix_out[None, :, None, :],
    )


def solution(mesh):
    placed = (
        P("dp", "group", "head", None),
        P("dp", "group", None, "head"),
        P("dp", "group", None, "head", None),
        P("dp", "group", None, "head"),
        P("dp", "group"),
        P("dp", "group"),
        P("dp", "group", None),
    )
    return jax.shard_map(
        body,
        mesh=mesh,
        in_specs=placed,
        out_specs=(
            P("dp", "group", "head", None, None),
            P("dp", "group", None, "head"),
            P("dp", "group", None, "head", None),
            P("dp", "group", "head", None),
        ),
        check_vma=False,
    )
```

time: 86.1 us -> 72.9 us (0.85)
  local copies, waits for them, and re-layouts: 6.63 us -> 0 us
  Pallas kernels: 77.2 us -> 70.8 us
    pallas_call x1, Pallas kernels: 77.2 us -> 57 us  [body(): pl.pallas_call(functools.partial(kernel, (dps, groups, kvh, hd, slots, nh...]
    pallas_call x0 -> x1, Pallas kernels: none -> 13.8 us  [body(): pl.pallas_call(hand_over, out_shape=tuple((jax.ShapeDtypeStruct(x.shape,...]
    unnamed x14 -> x0, local copies, waits for them, and re-layouts: 6.63 us -> none
where the time goes in v2:
time: 72.9 us; the launch traced here: 72.7 us
  Pallas kernels  70.8 us (97%)
  between operations  1.93 us (3%)
    pallas_call x1, Pallas kernels, body(): pl.pallas_call(functools.partial(kernel, (dps, groups, kvh, hd, slots, nh...  57 us
    pallas_call x1, Pallas kernels, body(): pl.pallas_call(hand_over, out_shape=tuple((jax.ShapeDtypeStruct(x.shape,...  13.8 us

profile of v2, /device:TPU:1, one launch (start us, length us, event | category | flops | bytes accessed | tf_op | source)
XLA Modules:
  0.0 72.7 jit_solution(17774062821074772275)
XLA Ops:
  1.9 57.0 %shared_prompt_attention.1 = (bf16[4,4,5120]{2,1,0:T(4,128)(2,1)}, bf16[128,640]{1,0:T(8,128)(2,1)}, bf16[128,256]{1,0:T(8,128)(2,1)}, bf16[48,256]{1,0:T(8,128)(2,1)}) custom-call(bf16[48,256]{1,0:T(8,128)(2,1)} %bitcast.12, bf16[128,640]{1,0:T(8,128)(2,1)} %bitcast.9, bf16[128,256]{1,0:T(8,128)(2,1)} %bitcast.11, bf16[128,640]{1,0:T(8,128)(2,1)} %bitcast.10, ...), custom_call_target="tpu_custom_call" | custom-call | tf_op jit(solution)/shard_map/shared_prompt_attention/pallas_call | solution.py:551
  58.9 13.8 %hand_over.1 = (bf16[4,4,5120]{2,1,0:T(4,128)(2,1)}, bf16[128,640]{1,0:T(8,128)(2,1)}, bf16[128,256]{1,0:T(8,128)(2,1)}, bf16[48,256]{1,0:T(8,128)(2,1)}) custom-call(bf16[4,4,5120]{2,1,0:T(4,128)(2,1)} %get-tuple-element.12.refs_0_, bf16[128,640]{1,0:T(8,128)(2,1)} %get-tuple-element.13.refs_1_, bf16[128,256]{1,0:T(8,128)(2,1)} %get-tuple-element.14.refs_2_, ...), custom_call_target="tpu_custom_call" | custom-call | tf_op jit(solution)/shard_map/hand_over/pallas_call | solution.py:611

commit v3 on v2

--- a/solution.py
+++ b/solution.py
@@ -524,11 +524,18 @@
 
 
 def hand_over(*refs):
-    count = (len(refs) - 1) // 2
-    copies = [pltpu.make_async_copy(refs[i], refs[count + i], refs[-1].at[i]) for i in range(count)]
-    for copy in copies:
+    count = (len(refs) - 1) // 3
+    sems = refs[-1]
+    inward = [pltpu.make_async_copy(refs[i], refs[2 * count + i], sems.at[0, i]) for i in range(count)]
+    outward = [
+        pltpu.make_async_copy(refs[2 * count + i], refs[count + i], sems.at[1, i]) for i in range(count)
+    ]
+    for copy in inward:
         copy.start()
-    for copy in copies:
+    for copy, following in zip(inward, outward):
+        copy.wait()
+        following.start()
+    for copy in outward:
         copy.wait()
 
 
@@ -613,7 +620,7 @@
         out_shape=tuple(jax.ShapeDtypeStruct(x.shape, x.dtype) for x in made),
         in_specs=[anywhere] * len(made),
         out_specs=(anywhere,) * len(made),
-        scratch_shapes=[dma((len(made),))],
+        scratch_shapes=[pltpu.VMEM(x.shape, x.dtype) for x in made] + [dma((2, len(made)))],
         compiler_params=pltpu.CompilerParams(vmem_limit_bytes=VMEM),
         name="hand_over",
     )(*made)

time: 72.9 us -> 60.9 us (0.84)
  Pallas kernels: 70.8 us -> 58.8 us
    pallas_call x1, Pallas kernels: 13.8 us -> 1.75 us  [body(): pl.pallas_call(hand_over, out_shape=tuple((jax.ShapeDtypeStruct(x.shape,...]
where the time goes in v3:
time: 60.9 us; the launch traced here: 60.7 us
  Pallas kernels  58.8 us (97%)
  between operations  1.93 us (3%)
    pallas_call x1, Pallas kernels, body(): pl.pallas_call(functools.partial(kernel, (dps, groups, kvh, hd, slots, nh...  57 us
    pallas_call x1, Pallas kernels, body(): pl.pallas_call(hand_over, out_shape=tuple((jax.ShapeDtypeStruct(x.shape,...  1.75 us

profile of v3, /device:TPU:1, one launch (start us, length us, event | category | flops | bytes accessed | tf_op | source)
XLA Modules:
  0.0 60.7 jit_solution(18326748033975201059)
XLA Ops:
  1.9 57.0 %shared_prompt_attention.1 = (bf16[4,4,5120]{2,1,0:T(4,128)(2,1)}, bf16[128,640]{1,0:T(8,128)(2,1)}, bf16[128,256]{1,0:T(8,128)(2,1)}, bf16[48,256]{1,0:T(8,128)(2,1)}) custom-call(bf16[48,256]{1,0:T(8,128)(2,1)} %bitcast.12, bf16[128,640]{1,0:T(8,128)(2,1)} %bitcast.9, bf16[128,256]{1,0:T(8,128)(2,1)} %bitcast.11, bf16[128,640]{1,0:T(8,128)(2,1)} %bitcast.10, ...), custom_call_target="tpu_custom_call" | custom-call | tf_op jit(solution)/shard_map/shared_prompt_attention/pallas_call | solution.py:558
  58.9 1.8 %hand_over.1 = (bf16[4,4,5120]{2,1,0:T(4,128)(2,1)}, bf16[128,640]{1,0:T(8,128)(2,1)}, bf16[128,256]{1,0:T(8,128)(2,1)}, bf16[48,256]{1,0:T(8,128)(2,1)}) custom-call(bf16[4,4,5120]{2,1,0:T(4,128)(2,1)} %get-tuple-element.12.refs_0_, bf16[128,640]{1,0:T(8,128)(2,1)} %get-tuple-element.13.refs_1_, bf16[128,256]{1,0:T(8,128)(2,1)} %get-tuple-element.14.refs_2_, ...), custom_call_target="tpu_custom_call" | custom-call | tf_op jit(solution)/shard_map/hand_over/pallas_call | solution.py:618

commit v4 on v2

--- a/solution.py
+++ b/solution.py
@@ -14,7 +14,7 @@
 NEAR = (5, -5, 3, -3, 2, -2, 1, -1)
 RELAY = 5
 FAR = 8
-VMEM = 64 * 2**20
+VMEM = 56 * 2**20
 
 
 def dot_nn(left, right):
@@ -252,14 +252,6 @@
         to_sibling(off, k).start()
     each(3, lambda i: lax.rem(i + chips - 1, chips))
 
-    for off, steps, far, half in ((5, (1, -1, 2, -2), 3, 0), (11, (-1, 1, -2, 2), -3, 1)):
-        arrived(off)
-        passed = [around(off, step) for step in steps] + [around(off, far, half)]
-        for copy in passed:
-            copy.start()
-        to_sibling(off, k).start()
-        sent += passed
-
     for copy in told:
         copy.wait_recv()
     window = facts + sc_recv[1] + sc_recv[2] + sc_recv[3] + sc_recv[4]
@@ -268,21 +260,27 @@
     told += [tell(6, 1, device(-5)), tell(7, 2, device(5))]
     for copy in told[5:]:
         copy.start()
+    for off, steps, far, half in ((5, (1, -1, 2, -2), 3, 0), (11, (-1, 1, -2, 2), -3, 1)):
+        arrived(off)
+        passed = [around(off, step) for step in steps] + [around(off, far, half)]
+        for copy in passed:
+            copy.start()
+        to_sibling(off, k).start()
+        sent += passed
+
     each(2, lambda i: 2 + 12 * i)
     each(2, lambda i: 5 + 6 * i)
 
-    for off in (4, 12, 6, 10, 3, 13, 7, 9):
+    for off in (4, 12, 6, 10, 3, 13, 7, 9, chips // 2):
         arrived(off)
         to_sibling(off, k).start()
-    each(4, lambda i: 4 + 2 * i + 2 * lax.div(i, 2))
-    arrived(chips // 2)
-    to_sibling(chips // 2, k).start()
     for copy in told[5:]:
         copy.wait_recv()
     window = window + sc_recv[6] + sc_recv[7]
     sc_send[3] = window
     told.append(tell(8, 3, sibling))
     told[7].start()
+    each(4, lambda i: 4 + 2 * i + 2 * lax.div(i, 2))
     each(4, lambda i: 3 + 4 * i - 2 * lax.div(i, 2))
     scores(chips // 2)
 
@@ -371,29 +369,6 @@
         step = 5 * lax.div(far + 5, 8) - far
         tree_send[side, far] = pair_sum(chips - far if side == 0 else far).astype(BF16)
         tree_copy(side, far, step if side == 0 else -step).start()
-
-    prepare(FAR)
-
-    def leaves(i, _):
-        for far in (7 - i, 3 + i):
-            prepare(chips - far)
-            prepare(far)
-
-        @pl.when(i == 0)
-        def _():
-            tree_send[0, FAR] = pair_sum(FAR).astype(BF16)
-            half_copy(0).start()
-            half_copy(1).start()
-
-        @pl.when(i == 1)
-        def _():
-            for far in (7, 3):
-                ship(far, 0)
-                ship(far, 1)
-
-        return 0
-
-    lax.fori_loop(0, 2, leaves, 0)
 
     to_row = lax.broadcasted_iota(jnp.int32, (slots, slots), 0)
     from_row = lax.broadcasted_iota(jnp.int32, (slots, slots), 1)
@@ -413,10 +388,6 @@
         for t in range(groups):
             a2a_send[t, :, cols] = moved[t * most : (t + 1) * most, :].astype(BF16)
 
-    for far in (6, 4):
-        ship(far, 0)
-        ship(far, 1)
-
     def place(c, hh):
         return packed.at[lax.rem(c, per), :, pl.ds(pl.multiple_of(hh * wide, wide), wide)]
 
@@ -445,7 +416,36 @@
 
         return 0
 
-    lax.fori_loop(0, groups, send_rows, 0)
+    lax.fori_loop(0, groups // 2, send_rows, 0)
+
+    prepare(FAR)
+
+    def leaves(i, _):
+        for far in (7 - i, 3 + i):
+            prepare(chips - far)
+            prepare(far)
+
+        @pl.when(i == 0)
+        def _():
+            tree_send[0, FAR] = pair_sum(FAR).astype(BF16)
+            half_copy(0).start()
+            half_copy(1).start()
+
+        @pl.when(i == 1)
+        def _():
+            for far in (7, 3):
+                ship(far, 0)
+                ship(far, 1)
+
+        return 0
+
+    lax.fori_loop(0, 2, leaves, 0)
+
+    for far in (6, 4):
+        ship(far, 0)
+        ship(far, 1)
+
+    lax.fori_loop(groups // 2, groups, send_rows, 0)
 
     def nearer(i, _):
         far = RELAY - 3 * lax.div(i + 1, 2) - lax.div(i, 2)
@@ -548,13 +548,17 @@
     vmem = pl.BlockSpec(memory_space=pltpu.VMEM)
     anywhere = pl.BlockSpec(memory_space=pl.ANY)
     dma = pltpu.SemaphoreType.DMA
+
+    def in_hbm(array):
+        return pltpu.with_memory_space_constraint(array, pltpu.HBM)
+
     made = pl.pallas_call(
         functools.partial(kernel, (dps, groups, kvh, hd, slots, nh)),
         out_shape=(
-            jax.ShapeDtypeStruct((per, most, kvh * wide), BF16),
-            jax.ShapeDtypeStruct((slots, wide), BF16),
-            jax.ShapeDtypeStruct((slots, 2 * hd), BF16),
-            jax.ShapeDtypeStruct((shard, 2 * hd), BF16),
+            pltpu.VMEM((per, most, kvh * wide), BF16),
+            pltpu.VMEM((slots, wide), BF16),
+            pltpu.VMEM((slots, 2 * hd), BF16),
+            pltpu.VMEM((shard, 2 * hd), BF16),
         ),
         in_specs=[anywhere] * 7,
         out_specs=(anywhere, vmem, vmem, vmem),
@@ -600,13 +604,13 @@
         ),
         name="shared_prompt_attention",
     )(
-        prefix_kv[0, :, 0, :],
-        comp_q[0, 0],
-        comp_kv[0, 0, :, 0, :],
-        grad_out[0, 0],
+        in_hbm(prefix_kv[0, :, 0, :]),
+        in_hbm(comp_q[0, 0]),
+        in_hbm(comp_kv[0, 0, :, 0, :]),
+        in_hbm(grad_out[0, 0]),
         rewards,
         lengths,
-        deal[0],
+        in_hbm(deal[0]),
     )
     packed, query_out, comp_out, prefix_out = pl.pallas_call(
         hand_over,
@@ -614,7 +618,7 @@
         in_specs=[anywhere] * len(made),
         out_specs=(anywhere,) * len(made),
         scratch_shapes=[dma((len(made),))],
-        compiler_params=pltpu.CompilerParams(vmem_limit_bytes=VMEM),
+        compiler_params=pltpu.CompilerParams(vmem_limit_bytes=8 * 2**20),
         name="hand_over",
     )(*made)
     return (

time: 72.9 us -> 56 us (0.77)
  Pallas kernels: 70.8 us -> 53.9 us
    pallas_call x1, Pallas kernels: 13.8 us -> 0.78 us  [body(): pl.pallas_call(hand_over, out_shape=tuple((jax.ShapeDtypeStruct(x.shape,...]
    pallas_call x1, Pallas kernels: 57 us -> 53.1 us  [body(): pl.pallas_call(functools.partial(kernel, (dps, groups, kvh, hd, slots, nh...]
where the time goes in v4:
time: 56 us; the launch traced here: 55.9 us
  Pallas kernels  53.9 us (96%)
  between operations  1.93 us (3%)
    pallas_call x1, Pallas kernels, body(): pl.pallas_call(functools.partial(kernel, (dps, groups, kvh, hd, slots, nh...  53.1 us

profile of v4, /device:TPU:1, one launch (start us, length us, event | category | flops | bytes accessed | tf_op | source)
XLA Modules:
  0.0 55.9 jit_solution(2181205202003171076)
XLA Ops:
  1.9 53.1 %shared_prompt_attention.1 = (bf16[4,4,5120]{2,1,0:T(4,128)(2,1)S(1)}, bf16[128,640]{1,0:T(8,128)(2,1)S(1)}, bf16[128,256]{1,0:T(8,128)(2,1)S(1)}, bf16[48,256]{1,0:T(8,128)(2,1)S(1)}) custom-call(bf16[48,256]{1,0:T(8,128)(2,1)} %bitcast.12, bf16[128,640]{1,0:T(8,128)(2,1)} %bitcast.9, bf16[128,256]{1,0:T(8,128)(2,1)} %bitcast.11, ...), custom_call_target="tpu_custom_call" | custom-call | tf_op jit(solution)/shard_map/shared_prompt_attention/pallas_call | solution.py:555
  55.1 0.8 %hand_over.1 = (bf16[4,4,5120]{2,1,0:T(4,128)(2,1)}, bf16[128,640]{1,0:T(8,128)(2,1)}, bf16[128,256]{1,0:T(8,128)(2,1)}, bf16[48,256]{1,0:T(8,128)(2,1)}) custom-call(bf16[4,4,5120]{2,1,0:T(4,128)(2,1)S(1)} %get-tuple-element.12.refs_0_, bf16[128,640]{1,0:T(8,128)(2,1)S(1)} %get-tuple-element.13.refs_1_, bf16[128,256]{1,0:T(8,128)(2,1)S(1)} %get-tuple-element.14.refs_2_, ...), custom_call_target="tpu_custom_call" | custom-call | tf_op jit(solution)/shard_map/hand_over/pallas_call | solution.py:615

commit v5 on v4

--- a/solution.py
+++ b/solution.py
@@ -15,6 +15,7 @@
 RELAY = 5
 FAR = 8
 VMEM = 56 * 2**20
+ROWS_FIRST, ROWS_EACH, ROWS_TURN, LAG = 12, 20, 15, 4
 
 
 def dot_nn(left, right):
@@ -64,6 +65,7 @@
     pair_recv,
     tree_send,
     tree_recv,
+    relayed,
     in_sems,
     ag_ss,
     ag_rs,
@@ -321,28 +323,28 @@
         value_grad = dot_nn(probs.astype(BF16), gs[...]) * weight
         return key_grad, value_grad
 
-    def pair_copy(off):
+    def pair_copy(owner):
         return pltpu.make_async_remote_copy(
-            src_ref=pair_send.at[off, pl.ds(pl.multiple_of((1 - k) * shard, shard), shard), :],
-            dst_ref=pair_recv.at[off],
-            send_sem=pair_ss.at[off],
-            recv_sem=pair_rs.at[off],
+            src_ref=pair_send.at[owner, pl.ds(pl.multiple_of((1 - k) * shard, shard), shard), :],
+            dst_ref=pair_recv.at[owner],
+            send_sem=pair_ss.at[owner],
+            recv_sem=pair_rs.at[owner],
             device_id=sibling,
             device_id_type=MESH,
         )
 
-    def prepare(off):
-        key_grad, value_grad = gradients(chunk_rows(chip(off)))
-        own[off, :, :hd] = key_grad
-        own[off, :, hd:] = value_grad
-        pair_send[off, :, :hd] = key_grad.astype(BF16)
-        pair_send[off, :, hd:] = value_grad.astype(BF16)
-        pair_copy(off).start()
-
-    def pair_sum(off):
-        pair_copy(off).wait_recv()
-        mine = own[off, pl.ds(pl.multiple_of(k * shard, shard), shard), :]
-        return mine + pair_recv[off].astype(F32)
+    def prepare(owner):
+        key_grad, value_grad = gradients(chunk_rows(owner))
+        own[owner, :, :hd] = key_grad
+        own[owner, :, hd:] = value_grad
+        pair_send[owner, :, :hd] = key_grad.astype(BF16)
+        pair_send[owner, :, hd:] = value_grad.astype(BF16)
+        pair_copy(owner).start()
+
+    def pair_sum(owner):
+        pair_copy(owner).wait_recv()
+        mine = own[owner, pl.ds(pl.multiple_of(k * shard, shard), shard), :]
+        return mine + pair_recv[owner].astype(F32)
 
     def tree_copy(side, far, step):
         return pltpu.make_async_remote_copy(
@@ -365,10 +367,22 @@
             device_id_type=MESH,
         )
 
-    def ship(far, side):
-        step = 5 * lax.div(far + 5, 8) - far
-        tree_send[side, far] = pair_sum(chips - far if side == 0 else far).astype(BF16)
-        tree_copy(side, far, step if side == 0 else -step).start()
+    def deliver(owner):
+        ahead = lax.rem(z - owner + chips, chips)
+        side = lax.div(ahead, FAR + 1)
+        far = ahead - side * (2 * ahead - chips)
+
+        @pl.when(far == FAR)
+        def _():
+            tree_send[0, FAR] = pair_sum(owner).astype(BF16)
+            half_copy(0).start()
+            half_copy(1).start()
+
+        @pl.when(jnp.logical_and(far != FAR, jnp.logical_and(far != 0, far != RELAY)))
+        def _():
+            step = 5 * lax.div(far + 5, 8) - far
+            tree_send[side, far] = pair_sum(owner).astype(BF16)
+            tree_copy(side, far, step * (1 - 2 * side)).start()
 
     to_row = lax.broadcasted_iota(jnp.int32, (slots, slots), 0)
     from_row = lax.broadcasted_iota(jnp.int32, (slots, slots), 1)
@@ -392,19 +406,17 @@
         return packed.at[lax.rem(c, per), :, pl.ds(pl.multiple_of(hh * wide, wide), wide)]
 
     def rows_copy(i):
-        j = lax.div(i + 1, 2)
-        t = lax.rem(g + groups // 2 + j * (1 - 2 * lax.rem(i, 2)), groups)
         return pltpu.make_async_remote_copy(
-            src_ref=a2a_send.at[t],
+            src_ref=a2a_send.at[i],
             dst_ref=place(g, h),
             send_sem=a2a_ss,
             recv_sem=a2a_rs,
-            device_id=(p, t, seat),
+            device_id=(p, i, seat),
             device_id_type=MESH,
         )
 
     def send_rows(i, _):
-        mine = jnp.logical_and(i == groups - 1, seat == h)
+        mine = jnp.logical_and(i == g, seat == h)
 
         @pl.when(mine)
         def _():
@@ -416,67 +428,50 @@
 
         return 0
 
-    lax.fori_loop(0, groups // 2, send_rows, 0)
-
-    prepare(FAR)
-
-    def leaves(i, _):
-        for far in (7 - i, 3 + i):
-            prepare(chips - far)
-            prepare(far)
-
-        @pl.when(i == 0)
+    lax.fori_loop(0, ROWS_FIRST, send_rows, 0)
+
+    def turn(owner, _):
+        prepare(owner)
+
+        @pl.when(owner >= LAG)
         def _():
-            tree_send[0, FAR] = pair_sum(FAR).astype(BF16)
-            half_copy(0).start()
-            half_copy(1).start()
-
-        @pl.when(i == 1)
-        def _():
-            for far in (7, 3):
-                ship(far, 0)
-                ship(far, 1)
-
+            deliver(owner - LAG)
+
+        first = jnp.minimum(ROWS_FIRST + ROWS_EACH * jnp.maximum(owner - ROWS_TURN, 0), groups)
+        past = jnp.minimum(ROWS_FIRST + ROWS_EACH * jnp.maximum(owner + 1 - ROWS_TURN, 0), groups)
+        lax.fori_loop(first, past, send_rows, 0)
         return 0
 
-    lax.fori_loop(0, 2, leaves, 0)
-
-    for far in (6, 4):
-        ship(far, 0)
-        ship(far, 1)
-
-    lax.fori_loop(groups // 2, groups, send_rows, 0)
-
-    def nearer(i, _):
-        far = RELAY - 3 * lax.div(i + 1, 2) - lax.div(i, 2)
-        prepare(chips - far)
-        prepare(far)
-
-        @pl.when(i == 2)
-        def _():
-            ship(2, 0)
-            ship(2, 1)
-
+    lax.fori_loop(0, chips, turn, 0)
+
+    def late(owner, _):
+        deliver(owner)
         return 0
 
-    lax.fori_loop(0, 3, nearer, 0)
-    ship(1, 0)
-    ship(1, 1)
-    prepare(0)
-
-    for side in range(2):
-        term = pair_sum(chips - RELAY if side == 0 else RELAY)
+    lax.fori_loop(chips - LAG, chips, late, 0)
+
+    lower = lax.div(z + RELAY, chips) + lax.div(chips + RELAY - 1 - z, chips)
+
+    def relay(i, _):
+        side = lax.rem(lower + i, 2)
+        term = pair_sum(lax.rem(z - RELAY + 2 * RELAY * side + chips, chips))
         for far in (7, 6, 4, 3):
             tree_copy(side, far, 1).wait_recv()
             term = term + tree_recv[side, far].astype(F32)
-        half_copy(side).wait_recv()
-        lanes = slice(side * hd, (side + 1) * hd)
-        rest = slice((1 - side) * hd, (2 - side) * hd)
-        tree_send[side, RELAY, :, lanes] = (
-            term[:, lanes] + tree_recv[side, FAR, :, lanes].astype(F32)
-        ).astype(BF16)
-        tree_send[side, RELAY, :, rest] = term[:, rest].astype(BF16)
-        tree_copy(side, RELAY, -5 if side == 0 else 5).start()
+        relayed[...] = term
+        for half in range(2):
+            lanes = slice(half * hd, (half + 1) * hd)
+
+            @pl.when(side == half)
+            def _():
+                half_copy(half).wait_recv()
+                relayed[:, lanes] += tree_recv[half, FAR, :, lanes].astype(F32)
+
+        tree_send[side, RELAY] = relayed[...].astype(BF16)
+        tree_copy(side, RELAY, RELAY * (2 * side - 1)).start()
+        return 0
+
+    lax.fori_loop(0, 2, relay, 0)
 
     key_grad, value_grad = gradients(own_rows)
     query_grad = dot_tn(kv[:, :hd], dst[...]) * key_weight
@@ -507,7 +502,7 @@
     for side in range(2):
         half_copy(side).wait_send()
 
-    term = pair_sum(0)
+    term = pair_sum(z)
     for far in (2, 1, RELAY):
         for side in range(2):
             tree_copy(side, far, 1).wait_recv()
@@ -585,6 +580,7 @@
             pltpu.VMEM((chips, shard, 2 * hd), BF16),
             pltpu.VMEM((2, FAR + 1, shard, 2 * hd), BF16),
             pltpu.VMEM((2, FAR + 1, shard, 2 * hd), BF16),
+            pltpu.VMEM((shard, 2 * hd), F32),
             dma((7,)),
             dma((chips + 2,)),
             dma((chips + 2,)),

time: 56 us -> 54.4 us (0.971)
  Pallas kernels: 53.9 us -> 52.2 us
    pallas_call x1, Pallas kernels: 53.1 us -> 51.4 us  [body(): pl.pallas_call(functools.partial(kernel, (dps, groups, kvh, hd, slots, nh...]
where the time goes in v5:
time: 54.4 us; the launch traced here: 54.2 us
  Pallas kernels  52.2 us (96%)
  between operations  1.93 us (4%)
    pallas_call x1, Pallas kernels, body(): pl.pallas_call(functools.partial(kernel, (dps, groups, kvh, hd, slots, nh...  51.4 us

profile of v5, /device:TPU:1, one launch (start us, length us, event | category | flops | bytes accessed | tf_op | source)
XLA Modules:
  0.0 54.2 jit_solution(8523753152515974236)
XLA Ops:
  1.9 51.4 %shared_prompt_attention.1 = (bf16[4,4,5120]{2,1,0:T(4,128)(2,1)S(1)}, bf16[128,640]{1,0:T(8,128)(2,1)S(1)}, bf16[128,256]{1,0:T(8,128)(2,1)S(1)}, bf16[48,256]{1,0:T(8,128)(2,1)S(1)}) custom-call(bf16[48,256]{1,0:T(8,128)(2,1)} %bitcast.12, bf16[128,640]{1,0:T(8,128)(2,1)} %bitcast.9, bf16[128,256]{1,0:T(8,128)(2,1)} %bitcast.11, ...), custom_call_target="tpu_custom_call" | custom-call | tf_op jit(solution)/shard_map/shared_prompt_attention/pallas_call | solution.py:550
  53.4 0.8 %hand_over.1 = (bf16[4,4,5120]{2,1,0:T(4,128)(2,1)}, bf16[128,640]{1,0:T(8,128)(2,1)}, bf16[128,256]{1,0:T(8,128)(2,1)}, bf16[48,256]{1,0:T(8,128)(2,1)}) custom-call(bf16[4,4,5120]{2,1,0:T(4,128)(2,1)S(1)} %get-tuple-element.12.refs_0_, bf16[128,640]{1,0:T(8,128)(2,1)S(1)} %get-tuple-element.13.refs_1_, bf16[128,256]{1,0:T(8,128)(2,1)S(1)} %get-tuple-element.14.refs_2_, ...), custom_call_target="tpu_custom_call" | custom-call | tf_op jit(solution)/shard_map/hand_over/pallas_call | solution.py:611

commit v6 on v5

--- a/solution.py
+++ b/solution.py
@@ -15,7 +15,7 @@
 RELAY = 5
 FAR = 8
 VMEM = 56 * 2**20
-ROWS_FIRST, ROWS_EACH, ROWS_TURN, LAG = 12, 20, 15, 4
+ROWS_FIRST, ROWS_EACH, ROWS_TURN, LAG = 8, 32, 15, 3
 
 
 def dot_nn(left, right):
@@ -53,7 +53,6 @@
     gs,
     gt,
     st,
-    dpt,
     dst,
     top,
     acc,
@@ -228,7 +227,6 @@
     own_rows = pl.ds(prompt, slots)
     own_scores = jnp.where(key_at <= query_at, dot_nt(kv[own_rows, :hd], qs[...]), -1e30)
     st[own_rows, :] = own_scores
-    dpt[own_rows, :] = dot_nt(kv[own_rows, hd:], gs[...])
     top[...] = jnp.max(own_scores, axis=0, keepdims=True)
 
     def chunk_rows(zz):
@@ -240,7 +238,6 @@
         s = dot_nt(kv[rows, :hd], qs[...])
         st[rows, :] = s
         top[...] = jnp.maximum(top[...], jnp.max(s, axis=0, keepdims=True))
-        dpt[rows, :] = dot_nt(kv[rows, hd:], gs[...])
 
     def each(count, off_of):
         def one(i, _):
@@ -249,10 +246,13 @@
 
         lax.fori_loop(0, count, one, 0)
 
-    for off in (1, 15, 2, 14):
+    for off, steps, far, half in ((5, (2, -2, 1, -1), 3, 0), (11, (-2, 2, -1, 1), -3, 1)):
         arrived(off)
+        passed = [around(off, far, half)] + [around(off, step) for step in steps]
+        for copy in passed:
+            copy.start()
         to_sibling(off, k).start()
-    each(3, lambda i: lax.rem(i + chips - 1, chips))
+        sent += passed
 
     for copy in told:
         copy.wait_recv()
@@ -262,15 +262,11 @@
     told += [tell(6, 1, device(-5)), tell(7, 2, device(5))]
     for copy in told[5:]:
         copy.start()
-    for off, steps, far, half in ((5, (1, -1, 2, -2), 3, 0), (11, (-1, 1, -2, 2), -3, 1)):
+
+    for off in (1, 15, 2, 14):
         arrived(off)
-        passed = [around(off, step) for step in steps] + [around(off, far, half)]
-        for copy in passed:
-            copy.start()
         to_sibling(off, k).start()
-        sent += passed
-
-    each(2, lambda i: 2 + 12 * i)
+    each(5, lambda i: lax.rem(i + chips - 2, chips))
     each(2, lambda i: 5 + 6 * i)
 
     for off in (4, 12, 6, 10, 3, 13, 7, 9, chips // 2):
@@ -317,7 +313,7 @@
 
     def gradients(rows):
         probs = st[rows, :] * inverse
-        ds = (probs * (dpt[rows, :] - delta)).astype(BF16)
+        ds = (probs * (dot_nt(kv[rows, hd:], gs[...]) - delta)).astype(BF16)
         dst[rows, :] = ds
         key_grad = dot_nn(ds, qs[...]) * key_weight
         value_grad = dot_nn(probs.astype(BF16), gs[...]) * weight
@@ -567,7 +563,6 @@
             pltpu.VMEM((nh * slots, hd), BF16),
             pltpu.VMEM((nh * slots, hd), BF16),
             pltpu.VMEM((hd, nh * slots), F32),
-            pltpu.VMEM((keys, nh * slots), F32),
             pltpu.VMEM((keys, nh * slots), F32),
             pltpu.VMEM((keys, nh * slots), BF16),
             pltpu.VMEM((1, nh * slots), F32),

time: 54.4 us -> 55.3 us (1.017)
  Pallas kernels: 52.2 us -> 52.9 us
    pallas_call x1, Pallas kernels: 51.4 us -> 52.2 us  [body(): pl.pallas_call(functools.partial(kernel, (dps, groups, kvh, hd, slots, nh...]
where the time goes in v6:
time: 55.3 us; the launch traced here: 54.9 us
  Pallas kernels  52.9 us (96%)
  between operations  1.93 us (3%)
    pallas_call x1, Pallas kernels, body(): pl.pallas_call(functools.partial(kernel, (dps, groups, kvh, hd, slots, nh...  52.2 us

profile of v6, /device:TPU:1, one launch (start us, length us, event | category | flops | bytes accessed | tf_op | source)
XLA Modules:
  0.0 54.9 jit_solution(6477211023695231638)
XLA Ops:
  1.9 52.2 %shared_prompt_attention.1 = (bf16[4,4,5120]{2,1,0:T(4,128)(2,1)S(1)}, bf16[128,640]{1,0:T(8,128)(2,1)S(1)}, bf16[128,256]{1,0:T(8,128)(2,1)S(1)}, bf16[48,256]{1,0:T(8,128)(2,1)S(1)}) custom-call(bf16[48,256]{1,0:T(8,128)(2,1)} %bitcast.12, bf16[128,640]{1,0:T(8,128)(2,1)} %bitcast.9, bf16[128,256]{1,0:T(8,128)(2,1)} %bitcast.11, ...), custom_call_target="tpu_custom_call" | custom-call | tf_op jit(solution)/shard_map/shared_prompt_attention/pallas_call | solution.py:546
  54.1 0.8 %hand_over.1 = (bf16[4,4,5120]{2,1,0:T(4,128)(2,1)}, bf16[128,640]{1,0:T(8,128)(2,1)}, bf16[128,256]{1,0:T(8,128)(2,1)}, bf16[48,256]{1,0:T(8,128)(2,1)}) custom-call(bf16[4,4,5120]{2,1,0:T(4,128)(2,1)S(1)} %get-tuple-element.12.refs_0_, bf16[128,640]{1,0:T(8,128)(2,1)S(1)} %get-tuple-element.13.refs_1_, bf16[128,256]{1,0:T(8,128)(2,1)S(1)} %get-tuple-element.14.refs_2_, ...), custom_call_target="tpu_custom_call" | custom-call | tf_op jit(solution)/shard_map/hand_over/pallas_call | solution.py:606
